TPU v7x, 32 devices: a whole 2x2x4 slice. The times are simulated.
32 devices in a mesh: groups: 2 (over y), exp: 4 (over z), patch: 2 (over x), band: 2 (over core).
Axes of the slice: x: 2, y: 2, z: 4, core: 2. Of those that a mesh axis runs over, the one named last changes fastest.
Arguments:
- templates: bfloat16 [8, 8, 256, 256], P(('groups', 'exp'), 'patch', None, 'band'), parts along dimension 0, may hold values from -6 to 6
- exposures: bfloat16 [8, 4, 4, 256, 256], P(('groups', 'exp'), 'patch', None, None, 'band'), parts along dimension 0, may hold values from -6 to 6
- variance: float32 [8, 4, 4, 256, 256], P(('groups', 'exp'), 'patch', None, None, 'band'), parts along dimension 0, may hold values from 0.5 to 4
- coefficients: float32 [8, 4, 4, 27], P(('groups', 'exp'), 'patch'), parts along dimension 0, may hold values from -1.2 to 1.2
- psf_width: float32 [8, 4, 4, 2], P(('groups', 'exp'), 'patch'), parts along dimension 0, may hold values from 1 to 2.5
- patch_ids: int32 [8, 4, 4], P(('groups', 'exp'), 'patch'), parts along dimension 0, may hold values from 0 to 23
- live_count: int32 [8, 4], P(('groups', 'exp'), 'patch'), parts along dimension 0, may hold values from 1 to 4
Outputs:
- coadd_diff: float32 [8, 8, 256, 256], P(('groups', 'exp'), 'patch', None, 'band'), parts along dimension 0
- score: float32 [8, 4, 4, 256, 256], P(('groups', 'exp'), 'patch', None, None, 'band'), parts along dimension 0
There are 2 independent parts, one for each index of `groups`. A program takes and returns all parts, laid end to end along the dimension named above; each array names one. Nothing has to cross between parts.
Inputs may be any that keep to these rules, and one draw needn't show every extreme that they name: `patch_ids`: an id names patch id % 8 of the grid row id // 8 - 1 relative to the exposure's own row. `live_count`: sub-tiles at slots below the count are live.
All inputs are finite; a program needn't handle non-finite values.
Results may differ from a plain program's by a relative error of at most 0.0049.
Values may be sent and summed in bfloat16 or wider, within the bound.
A program may use at most 64 MiB of HBM per device.

v0:
```python
import jax
import jax.numpy as jnp
import numpy as np
from jax import lax
from jax.sharding import PartitionSpec as P

NB = 27
HW = 10
PW = 7


sigmas = (0.75, 1.5, 3.0)
degrees = (4, 2, 2)


def with_halo(value, sides, width):
    for axis, dim in sides:
        devices, length = (lax.axis_size(axis), value.shape[dim])
        up = [(i, (i + 1) % devices) for i in range(devices - 1)]
        down = [(j, i) for i, j in up]
        last = lax.slice_in_dim(value, length - width, length, axis=dim)
        first = lax.slice_in_dim(value, 0, width, axis=dim)
        before = lax.ppermute(last, axis, up)
        after = lax.ppermute(first, axis, down)
        value = jnp.concatenate([before, value, after], axis=dim)
    return value


def shifted(block, axis, distance):
    devices = range(lax.axis_size(axis))
    route = [(i - distance, i) for i in devices if i - distance in devices]
    return lax.ppermute(block, axis, route)


def basis_terms():
    terms = []
    offset = 0
    for group in range(3):
        for first in range(degrees[group] + 1):
            for second in range(degrees[group] + 1 - first):
                terms.append((group, first, second, offset + first))
        offset = offset + degrees[group] + 1
    return terms


def membership():
    table = np.zeros((27, 11), np.float32)
    for index, term in enumerate(basis_terms()):
        table[index, term[3]] = 1.0
    return table


def profile(offset, sigma, power, reach):
    grid = jnp.arange(-reach, reach + 1).astype(jnp.float32)
    base = jnp.exp(-grid * grid / (2.0 * sigma * sigma)) * (grid / reach) ** power
    scale = jnp.sqrt(jnp.sum(base * base))
    spot = offset.astype(jnp.float32)
    value = jnp.exp(-spot * spot / (2.0 * sigma * sigma)) * (spot / reach) ** power / scale
    return jnp.where(jnp.abs(offset) <= reach, value, jnp.zeros_like(value))


def row_tables(count, reach):
    index = jnp.arange(count, dtype=jnp.int32)
    offset = index[:, None] - index[None, :]
    tables = []
    for group in range(3):
        for first in range(degrees[group] + 1):
            tables.append(profile(offset, sigmas[group], first, reach))
    return jnp.stack(tables).astype(jnp.bfloat16)


def column_tables(cols_in, cols_out, shift, reach):
    inner = jnp.arange(cols_in, dtype=jnp.int32)[:, None]
    outer = jnp.arange(cols_out, dtype=jnp.int32)[None, :]
    offset = outer + shift - inner
    return jnp.stack([profile(offset, sigmas[term[0]], term[2], reach) for term in basis_terms()])


def psf_table(offset, width, reach):
    grid = jnp.arange(-reach, reach + 1).astype(jnp.float32)
    total = jnp.sum(jnp.exp(-grid * grid / (2.0 * width * width)))
    spot = offset.astype(jnp.float32)
    value = jnp.exp(-spot * spot / (2.0 * width * width)) / total
    return jnp.where(jnp.abs(offset) <= reach, value, jnp.zeros_like(value))


def on_device(templates, exposures, variance, coefficients, psf_width, patch_ids, live_count):
    size = templates.shape[2]
    cols = templates.shape[3]
    owned = templates.shape[1]
    slots = patch_ids.shape[2]
    grid_row = lax.all_gather(templates, "patch", axis=1, tiled=True)
    window = with_halo(grid_row, (("exp", 0),), 1)
    patches_row = window.shape[1]
    flat_window = window.reshape(3 * patches_row, size, cols)
    ids = patch_ids.reshape(-1)
    chosen = jnp.take(flat_window, ids, axis=0)
    padded = with_halo(chosen, (("band", 2),), HW)
    gr_flat = row_tables(size, HW).reshape(-1, size)
    col_tab = column_tables(cols + 2 * HW, cols, HW, HW)
    member = jnp.asarray(membership())
    live = (
        (jnp.arange(slots, dtype=jnp.int32)[None, None, :] < live_count[:, :, None])
        .astype(jnp.float32)
        .reshape(-1)
    )
    exp_flat = exposures.reshape(-1, size, cols)
    var_flat = variance.reshape(-1, size, cols)

    def convolve(items):
        template, coeff, exposure, var_tile = items
        rows = (
            jnp.dot(gr_flat, template, preferred_element_type=jnp.float32)
            .astype(jnp.bfloat16)
            .reshape(11, size, cols + 2 * HW)
        )
        mixing = coeff[:, None] * member
        mats = jnp.einsum("kp,kcd->pcd", mixing, col_tab, precision=lax.Precision.HIGHEST).astype(
            jnp.bfloat16
        )
        convolved = jnp.einsum("psc,pcd->sd", rows, mats, preferred_element_type=jnp.float32)
        weight = 1.0 / var_tile
        return ((exposure.astype(jnp.float32) - convolved) * weight, weight.astype(jnp.bfloat16))

    weighted, inverse_low = lax.map(
        convolve, (padded, coefficients.reshape(-1, NB), exp_flat, var_flat)
    )
    stacked = jnp.stack([weighted.astype(jnp.bfloat16), inverse_low])
    widened = with_halo(stacked, (("band", 3),), PW)
    index = jnp.arange(size, dtype=jnp.int32)
    offset_rows = index[:, None] - index[None, :]
    offset_cols = (
        jnp.arange(cols, dtype=jnp.int32)[None, :]
        + PW
        - jnp.arange(cols + 2 * PW, dtype=jnp.int32)[:, None]
    )

    def matched(items):
        weighted_pad, inverse_pad, width, alive = items
        prow = psf_table(offset_rows, width[0], PW)
        pcol = psf_table(offset_cols, width[1], PW)
        numer = jnp.dot(
            prow.astype(jnp.bfloat16), weighted_pad, preferred_element_type=jnp.float32
        ).astype(jnp.bfloat16)
        numer = jnp.dot(numer, pcol.astype(jnp.bfloat16), preferred_element_type=jnp.float32)
        denom = jnp.dot(
            (prow * prow).astype(jnp.bfloat16), inverse_pad, preferred_element_type=jnp.float32
        ).astype(jnp.bfloat16)
        denom = jnp.dot(
            denom, (pcol * pcol).astype(jnp.bfloat16), preferred_element_type=jnp.float32
        )
        return alive * numer / jnp.sqrt(denom)

    score = lax.map(matched, (widened[0], widened[1], psf_width.reshape(-1, 2), live))
    masked = weighted * live[:, None, None]
    onehot = (ids[:, None] == jnp.arange(3 * patches_row, dtype=jnp.int32)[None, :]).astype(
        jnp.float32
    )
    partial_value = jnp.einsum(
        "nq,nsc->qsc", onehot, masked, precision=lax.Precision.HIGHEST
    ).reshape(3, patches_row, size, cols)
    from_below = shifted(partial_value[2].astype(jnp.bfloat16), "exp", 1).astype(jnp.float32)
    from_above = shifted(partial_value[0].astype(jnp.bfloat16), "exp", -1).astype(jnp.float32)
    row_total = partial_value[1] + from_below + from_above
    coadd = lax.psum_scatter(row_total, "patch", scatter_dimension=0, tiled=True)
    return (coadd.reshape(1, owned, size, cols), score.reshape(exposures.shape))


def solution(mesh):
    in_specs = (
        P(("groups", "exp"), "patch", None, "band"),
        P(("groups", "exp"), "patch", None, None, "band"),
        P(("groups", "exp"), "patch", None, None, "band"),
        P(("groups", "exp"), "patch", None, None),
        P(("groups", "exp"), "patch", None, None),
        P(("groups", "exp"), "patch", None),
        P(("groups", "exp"), "patch"),
    )
    out_specs = (
        P(("groups", "exp"), "patch", None, "band"),
        P(("groups", "exp"), "patch", None, None, "band"),
    )
    return jax.shard_map(
        on_device, mesh=mesh, in_specs=in_specs, out_specs=out_specs, check_vma=False
    )
```

profile of v0, /device:TPU:0, one launch (start us, length us, event | category | flops | bytes accessed | tf_op | source)
XLA Modules:
  0.0 269.9 jit_solution(12794665926467850008)
XLA Ops:
  7.2 10.2 %all_gather.3 = bf16[1,8,256,128]{3,2,0,1:T(8,128)(2,1)S(1)} all-gather(bf16[1,4,256,128]{3,2,0,1:T(8,128)(2,1)} %bitcast.122), channel_id=1, replica_groups=mesh['groups'=2,'exp'=4,'patch'=2,'band'=2] {'patch'}, dimensions={1}, use_global_device_ids=true | all-gather | bytes 786432 | tf_op jit(solution)/shard_map/all_gather | solution.py:92
  17.4 3.7 %collective-permute-start = (bf16[1,8,256,128]{3,2,1,0:T(8,128)(2,1)S(1)}, bf16[1,8,256,128]{3,2,1,0:T(8,128)(2,1)S(1)}, u32[]{:S(2)}, u32[]{:S(2)}) collective-permute-start(bf16[1,8,256,128]{3,2,1,0:T(8,128)(2,1)S(1)} %bitcast.117), channel_id=1, source_target_pairs={{0,4},{4,8},{8,12},{1,5},{5,9},{9,13},{2,6},{6,10},{10,14},{3,7},{... | collective-permute-start | bytes 1572872 | tf_op jit(solution)/shard_map/ppermute | solution.py:23
  53.1 10.2 %stack.12 = f32[27,148,128]{2,0,1:T(8,128)S(1)} concatenate(f32[1,148,128]{2,0,1:T(1,128)S(1)} %get-tuple-element.312, f32[1,148,128]{2,0,1:T(1,128)S(1)} %get-tuple-element.313, f32[1,148,128]{2,0,1:T(1,128)S(1)} %get-tuple-element.314, f32[1,148,128]{2,0,1:T(1,128)S(1)} %get-tuple-element.305, f32[1,148,128]{2,0,1:T(1,128)} %get-tuple-element.306, ...), dimensions={0} | concatenate | bytes 4091904 | tf_op jit(solution)/shard_map/stack | solution.py:76
  63.3 2.8 %pad_maximum_fusion.2 = bf16[8,256,148]{2,1,0:T(8,128)(2,1)} fusion(bf16[8,256,10]{2,1,0:T(8,128)(2,1)} %collective-permute-done.3, bf16[8,256,128]{2,1,0:T(8,128)(2,1)S(1)} %broadcast_select_fusion, bf16[8,256,10]{2,1,0:T(8,128)(2,1)} %collective-permute-done.2), kind=kLoop, calls=%fused_computation.66 | loop fusion | flops 1818624 | bytes 1212416 | tf_op jit(solution)/shard_map/concatenate | solution.py:25
  67.2 82.3 %while.27 = (s32[]{:T(128)}, f32[8,256,128]{2,1,0:T(8,128)}, bf16[8,256,128]{2,1,0:T(8,128)(2,1)}, bf16[8,256,128]{2,1,0:T(8,128)(2,1)}, bf16[8,256,148]{2,1,0:T...) while((s32[]{:T(128)}, f32[8,256,128]{2,1,0:T(8,128)}, ...), condition=%wide.region_12.13_spmd.clone, body=%wide.region_11.12_spmd.sunk.clone.sunk | while | flops 388416288 | bytes 14649461 | solution.py:125
  73.1 2.9 %fusion.127 = f32[8,256,128]{2,1,0:T(8,128)} fusion(f32[8,256,128]{2,1,0:T(8,128)} %get-tuple-element.435, s32[]{:T(128)} %get-tuple-element.434, bf16[11,256,148]{1,0,2:T(8,128)(2,1)} %reshape.773, bf16[11,148,128]{2,0,1:T(8,128)(2,1)} %convolution_convert_fusion.5, bf16[8,256,128]{2,1,0:T(8,128)(2,1)} %get-tuple-element.448, ...), kind=kOutput, calls=%fused_computation.12.clone.1 | convolution fusion | flops 106823680 | bytes 2146816 | tf_op jit(solution)/shard_map/while/body/eval_jaxpr/psc,pcd->sd/dot_general | solution.py:121
  83.3 2.9 %fusion.127 = f32[8,256,128]{2,1,0:T(8,128)} fusion(f32[8,256,128]{2,1,0:T(8,128)} %get-tuple-element.435, s32[]{:T(128)} %get-tuple-element.434, bf16[11,256,148]{1,0,2:T(8,128)(2,1)} %reshape.773, bf16[11,148,128]{2,0,1:T(8,128)(2,1)} %convolution_convert_fusion.5, bf16[8,256,128]{2,1,0:T(8,128)(2,1)} %get-tuple-element.448, ...), kind=kOutput, calls=%fused_computation.12.clone.1 | convolution fusion | flops 106823680 | bytes 2146816 | tf_op jit(solution)/shard_map/while/body/eval_jaxpr/psc,pcd->sd/dot_general | solution.py:121
  93.6 2.9 %fusion.127 = f32[8,256,128]{2,1,0:T(8,128)} fusion(f32[8,256,128]{2,1,0:T(8,128)} %get-tuple-element.435, s32[]{:T(128)} %get-tuple-element.434, bf16[11,256,148]{1,0,2:T(8,128)(2,1)} %reshape.773, bf16[11,148,128]{2,0,1:T(8,128)(2,1)} %convolution_convert_fusion.5, bf16[8,256,128]{2,1,0:T(8,128)(2,1)} %get-tuple-element.448, ...), kind=kOutput, calls=%fused_computation.12.clone.1 | convolution fusion | flops 106823680 | bytes 2146816 | tf_op jit(solution)/shard_map/while/body/eval_jaxpr/psc,pcd->sd/dot_general | solution.py:121
  103.9 2.9 %fusion.127 = f32[8,256,128]{2,1,0:T(8,128)} fusion(f32[8,256,128]{2,1,0:T(8,128)} %get-tuple-element.435, s32[]{:T(128)} %get-tuple-element.434, bf16[11,256,148]{1,0,2:T(8,128)(2,1)} %reshape.773, bf16[11,148,128]{2,0,1:T(8,128)(2,1)} %convolution_convert_fusion.5, bf16[8,256,128]{2,1,0:T(8,128)(2,1)} %get-tuple-element.448, ...), kind=kOutput, calls=%fused_computation.12.clone.1 | convolution fusion | flops 106823680 | bytes 2146816 | tf_op jit(solution)/shard_map/while/body/eval_jaxpr/psc,pcd->sd/dot_general | solution.py:121
  114.2 2.9 %fusion.127 = f32[8,256,128]{2,1,0:T(8,128)} fusion(f32[8,256,128]{2,1,0:T(8,128)} %get-tuple-element.435, s32[]{:T(128)} %get-tuple-element.434, bf16[11,256,148]{1,0,2:T(8,128)(2,1)} %reshape.773, bf16[11,148,128]{2,0,1:T(8,128)(2,1)} %convolution_convert_fusion.5, bf16[8,256,128]{2,1,0:T(8,128)(2,1)} %get-tuple-element.448, ...), kind=kOutput, calls=%fused_computation.12.clone.1 | convolution fusion | flops 106823680 | bytes 2146816 | tf_op jit(solution)/shard_map/while/body/eval_jaxpr/psc,pcd->sd/dot_general | solution.py:121
  124.5 2.9 %fusion.127 = f32[8,256,128]{2,1,0:T(8,128)} fusion(f32[8,256,128]{2,1,0:T(8,128)} %get-tuple-element.435, s32[]{:T(128)} %get-tuple-element.434, bf16[11,256,148]{1,0,2:T(8,128)(2,1)} %reshape.773, bf16[11,148,128]{2,0,1:T(8,128)(2,1)} %convolution_convert_fusion.5, bf16[8,256,128]{2,1,0:T(8,128)(2,1)} %get-tuple-element.448, ...), kind=kOutput, calls=%fused_computation.12.clone.1 | convolution fusion | flops 106823680 | bytes 2146816 | tf_op jit(solution)/shard_map/while/body/eval_jaxpr/psc,pcd->sd/dot_general | solution.py:121
  134.8 2.9 %fusion.127 = f32[8,256,128]{2,1,0:T(8,128)} fusion(f32[8,256,128]{2,1,0:T(8,128)} %get-tuple-element.435, s32[]{:T(128)} %get-tuple-element.434, bf16[11,256,148]{1,0,2:T(8,128)(2,1)} %reshape.773, bf16[11,148,128]{2,0,1:T(8,128)(2,1)} %convolution_convert_fusion.5, bf16[8,256,128]{2,1,0:T(8,128)(2,1)} %get-tuple-element.448, ...), kind=kOutput, calls=%fused_computation.12.clone.1 | convolution fusion | flops 106823680 | bytes 2146816 | tf_op jit(solution)/shard_map/while/body/eval_jaxpr/psc,pcd->sd/dot_general | solution.py:121
  145.1 2.9 %fusion.127 = f32[8,256,128]{2,1,0:T(8,128)} fusion(f32[8,256,128]{2,1,0:T(8,128)} %get-tuple-element.435, s32[]{:T(128)} %get-tuple-element.434, bf16[11,256,148]{1,0,2:T(8,128)(2,1)} %reshape.773, bf16[11,148,128]{2,0,1:T(8,128)(2,1)} %convolution_convert_fusion.5, bf16[8,256,128]{2,1,0:T(8,128)(2,1)} %get-tuple-element.448, ...), kind=kOutput, calls=%fused_computation.12.clone.1 | convolution fusion | flops 106823680 | bytes 2146816 | tf_op jit(solution)/shard_map/while/body/eval_jaxpr/psc,pcd->sd/dot_general | solution.py:121
  156.1 5.3 %collective-permute-start.4 = (bf16[8,256,128]{2,0,1:T(8,128)(2,1)}, bf16[8,256,128]{2,0,1:T(8,128)(2,1)}, u32[]{:S(2)}, u32[]{:S(2)}) collective-permute-start(bf16[8,256,128]{2,0,1:T(8,128)(2,1)} %get-tuple-element.296), channel_id=1, source_target_pairs={{0,4},{4,8},{8,12},{1,5},{5,9},{9,13},{2,6},{6,10},{10,14},{3,7},{... | collective-permute-start | bytes 1572872 | tf_op jit(solution)/shard_map/ppermute | solution.py:32
  162.8 3.4 %collective-permute-start.6 = (bf16[2,8,256,7]{2,1,3,0:T(8,128)(2,1)S(1)}, bf16[2,8,256,7]{2,1,3,0:T(8,128)(2,1)S(1)}, u32[]{:S(2)}, u32[]{:S(2)}) collective-permute-start(bf16[2,8,256,7]{2,1,3,0:T(8,128)(2,1)S(1)} %get-tuple-element.300), channel_id=1, source_target_pairs={{0,1},{2,3},{4,5},{6,7},{8,9},{10,11},{12,13},{14,15},{16,17},{18,... | collective-permute-start | bytes 172040 | tf_op jit(solution)/shard_map/ppermute | solution.py:23
  175.1 2.9 %collective-permute-done.5 = bf16[8,256,128]{2,0,1:T(8,128)(2,1)} collective-permute-done((bf16[8,256,128]{2,0,1:T(8,128)(2,1)}, bf16[8,256,128]{2,0,1:T(8,128)(2,1)}, u32[]{:S(2)}, u32[]{:S(2)}) %collective-permute-start.5) | collective-permute-done | bytes 524320 | tf_op jit(solution)/shard_map/ppermute | solution.py:32
  180.7 81.4 %while.28 = (s32[]{:T(128)}, f32[8,256,128]{2,1,0:T(8,128)S(1)}, f32[8]{0:T(128)S(1)}, f32[8,2]{0,1:T(2,128)S(1)}, bf16[8,256,142]{2,1,0:T(8,128)(2,1)}, /*index...) while((s32[]{:T(128)}, f32[8,256,128]{2,1,0:T(8,128)S(1)}, ...), condition=%wide.region_17.18_spmd.clone.clone, body=%wide.region_14.17_spmd.clone.clone.sunk | while | flops 57732988 | bytes 660701 | solution.py:154
  185.0 3.2 %convolution_multiply_fusion.2 = f32[256,128]{1,0:T(8,128)S(1)} fusion(bf16[8,256,142]{2,1,0:T(8,128)(2,1)} %get-tuple-element.478, s32[]{:T(128)} %get-tuple-element.465, f32[]{:T(128)} %get-tuple-element.421, f32[]{:T(128)S(6)} %mul.999, f32[]{:T(128)} %bitcast.110, s32[128]{0:T(128)S(1)} %get-tuple-element.480, f32[]{:T(128)} %get-tuple-element.422, ...), kind=kOutput, calls=%fused_computation.29.clone.1 | convolution fusion | flops 28824576 | bytes 264712 | tf_op jit(solution)/shard_map/while/body/eval_jaxpr/dot_general | solution.py:145
  188.2 2.6 fusion.133
  195.2 3.2 %convolution_multiply_fusion.2 = f32[256,128]{1,0:T(8,128)S(1)} fusion(bf16[8,256,142]{2,1,0:T(8,128)(2,1)} %get-tuple-element.478, s32[]{:T(128)} %get-tuple-element.465, f32[]{:T(128)} %get-tuple-element.421, f32[]{:T(128)S(6)} %mul.999, f32[]{:T(128)} %bitcast.110, s32[128]{0:T(128)S(1)} %get-tuple-element.480, f32[]{:T(128)} %get-tuple-element.422, ...), kind=kOutput, calls=%fused_computation.29.clone.1 | convolution fusion | flops 28824576 | bytes 264712 | tf_op jit(solution)/shard_map/while/body/eval_jaxpr/dot_general | solution.py:145
  198.4 2.6 fusion.133
  205.4 3.2 %convolution_multiply_fusion.2 = f32[256,128]{1,0:T(8,128)S(1)} fusion(bf16[8,256,142]{2,1,0:T(8,128)(2,1)} %get-tuple-element.478, s32[]{:T(128)} %get-tuple-element.465, f32[]{:T(128)} %get-tuple-element.421, f32[]{:T(128)S(6)} %mul.999, f32[]{:T(128)} %bitcast.110, s32[128]{0:T(128)S(1)} %get-tuple-element.480, f32[]{:T(128)} %get-tuple-element.422, ...), kind=kOutput, calls=%fused_computation.29.clone.1 | convolution fusion | flops 28824576 | bytes 264712 | tf_op jit(solution)/shard_map/while/body/eval_jaxpr/dot_general | solution.py:145
  215.5 3.2 %convolution_multiply_fusion.2 = f32[256,128]{1,0:T(8,128)S(1)} fusion(bf16[8,256,142]{2,1,0:T(8,128)(2,1)} %get-tuple-element.478, s32[]{:T(128)} %get-tuple-element.465, f32[]{:T(128)} %get-tuple-element.421, f32[]{:T(128)S(6)} %mul.999, f32[]{:T(128)} %bitcast.110, s32[128]{0:T(128)S(1)} %get-tuple-element.480, f32[]{:T(128)} %get-tuple-element.422, ...), kind=kOutput, calls=%fused_computation.29.clone.1 | convolution fusion | flops 28824576 | bytes 264712 | tf_op jit(solution)/shard_map/while/body/eval_jaxpr/dot_general | solution.py:145
  218.7 2.6 fusion.133
  225.7 3.2 %convolution_multiply_fusion.2 = f32[256,128]{1,0:T(8,128)S(1)} fusion(bf16[8,256,142]{2,1,0:T(8,128)(2,1)} %get-tuple-element.478, s32[]{:T(128)} %get-tuple-element.465, f32[]{:T(128)} %get-tuple-element.421, f32[]{:T(128)S(6)} %mul.999, f32[]{:T(128)} %bitcast.110, s32[128]{0:T(128)S(1)} %get-tuple-element.480, f32[]{:T(128)} %get-tuple-element.422, ...), kind=kOutput, calls=%fused_computation.29.clone.1 | convolution fusion | flops 28824576 | bytes 264712 | tf_op jit(solution)/shard_map/while/body/eval_jaxpr/dot_general | solution.py:145
  228.9 2.6 fusion.133
  235.9 3.2 %convolution_multiply_fusion.2 = f32[256,128]{1,0:T(8,128)S(1)} fusion(bf16[8,256,142]{2,1,0:T(8,128)(2,1)} %get-tuple-element.478, s32[]{:T(128)} %get-tuple-element.465, f32[]{:T(128)} %get-tuple-element.421, f32[]{:T(128)S(6)} %mul.999, f32[]{:T(128)} %bitcast.110, s32[128]{0:T(128)S(1)} %get-tuple-element.480, f32[]{:T(128)} %get-tuple-element.422, ...), kind=kOutput, calls=%fused_computation.29.clone.1 | convolution fusion | flops 28824576 | bytes 264712 | tf_op jit(solution)/shard_map/while/body/eval_jaxpr/dot_general | solution.py:145
  239.1 2.6 fusion.133
  246.1 3.2 %convolution_multiply_fusion.2 = f32[256,128]{1,0:T(8,128)S(1)} fusion(bf16[8,256,142]{2,1,0:T(8,128)(2,1)} %get-tuple-element.478, s32[]{:T(128)} %get-tuple-element.465, f32[]{:T(128)} %get-tuple-element.421, f32[]{:T(128)S(6)} %mul.999, f32[]{:T(128)} %bitcast.110, s32[128]{0:T(128)S(1)} %get-tuple-element.480, f32[]{:T(128)} %get-tuple-element.422, ...), kind=kOutput, calls=%fused_computation.29.clone.1 | convolution fusion | flops 28824576 | bytes 264712 | tf_op jit(solution)/shard_map/while/body/eval_jaxpr/dot_general | solution.py:145
  249.3 2.6 fusion.133
  256.2 3.2 %convolution_multiply_fusion.2 = f32[256,128]{1,0:T(8,128)S(1)} fusion(bf16[8,256,142]{2,1,0:T(8,128)(2,1)} %get-tuple-element.478, s32[]{:T(128)} %get-tuple-element.465, f32[]{:T(128)} %get-tuple-element.421, f32[]{:T(128)S(6)} %mul.999, f32[]{:T(128)} %bitcast.110, s32[128]{0:T(128)S(1)} %get-tuple-element.480, f32[]{:T(128)} %get-tuple-element.422, ...), kind=kOutput, calls=%fused_computation.29.clone.1 | convolution fusion | flops 28824576 | bytes 264712 | tf_op jit(solution)/shard_map/while/body/eval_jaxpr/dot_general | solution.py:145
  259.4 2.6 fusion.133
  (178 shorter events, 123.0 us)
Async XLA Ops:
  7.2 254.9 %reduce-scatter.2.cloned.1.call-start = ((), (), s32[]{:S(2)}) async-start(), calls=%async_computation.1 | async-start | bytes 1572864 | tf_op jit(solution)/shard_map/reduce_scatter | solution.py:165
  17.4 24.9 %copy-start.5 = (bf16[1,8,256,128]{3,2,0,1:T(8,128)(2,1)}, bf16[1,8,256,128]{3,2,0,1:T(8,128)(2,1)S(1)}, u32[]{:S(2)}) copy-start(bf16[1,8,256,128]{3,2,0,1:T(8,128)(2,1)S(1)} %all_gather.3) | copy-start | bytes 1572868
  17.4 24.9 %collective-permute-start = (bf16[1,8,256,128]{3,2,1,0:T(8,128)(2,1)S(1)}, bf16[1,8,256,128]{3,2,1,0:T(8,128)(2,1)S(1)}, u32[]{:S(2)}, u32[]{:S(2)}) collective-permute-start(bf16[1,8,256,128]{3,2,1,0:T(8,128)(2,1)S(1)} %bitcast.117), channel_id=1, source_target_pairs={{0,4},{4,8},{8,12},{1,5},{5,9},{9,13},{2,6},{6,10},{10,14},{3,7},{... | collective-permute-start | bytes 1572872 | tf_op jit(solution)/shard_map/ppermute | solution.py:23
  21.1 22.0 %collective-permute-start.1 = (bf16[1,8,256,128]{3,2,1,0:T(8,128)(2,1)S(1)}, bf16[1,8,256,128]{3,2,1,0:T(8,128)(2,1)}, u32[]{:S(2)}, u32[]{:S(2)}) collective-permute-start(bf16[1,8,256,128]{3,2,1,0:T(8,128)(2,1)S(1)} %bitcast.118), channel_id=1, source_target_pairs={{4,0},{8,4},{12,8},{5,1},{9,5},{13,9},{6,2},{10,6},{14,10},{7,3},{... | collective-permute-start | bytes 1572872 | tf_op jit(solution)/shard_map/ppermute | solution.py:24
  42.3 0.8 copy-start.7
  46.0 6.0 %copy-start.9 = (f32[1,2,4,2]{2,3,1,0:T(2,128)S(1)}, f32[1,2,4,2]{2,3,1,0:T(2,128)}, u32[]{:S(2)}) copy-start(f32[1,2,4,2]{2,3,1,0:T(2,128)} %param.16) | copy-start | bytes 196
  48.4 15.0 %collective-permute-start.2 = (bf16[8,256,10]{2,1,0:T(8,128)(2,1)}, bf16[8,256,10]{2,1,0:T(8,128)(2,1)}, u32[]{:S(2)}, u32[]{:S(2)}) collective-permute-start(bf16[8,256,10]{2,1,0:T(8,128)(2,1)} %get-tuple-element.302), channel_id=1, source_target_pairs={{0,1},{2,3},{4,5},{6,7},{8,9},{10,11},{12,13},{14,15},{16,17},{18,... | collective-permute-start | bytes 122888 | tf_op jit(solution)/shard_map/ppermute | solution.py:23
  50.5 12.9 %collective-permute-start.3 = (bf16[8,256,10]{2,1,0:T(8,128)(2,1)}, bf16[8,256,10]{2,1,0:T(8,128)(2,1)}, u32[]{:S(2)}, u32[]{:S(2)}) collective-permute-start(bf16[8,256,10]{2,1,0:T(8,128)(2,1)} %get-tuple-element.303), channel_id=1, source_target_pairs={{1,0},{3,2},{5,4},{7,6},{9,8},{11,10},{13,12},{15,14},{17,16},{19,... | collective-permute-start | bytes 122888 | tf_op jit(solution)/shard_map/ppermute | solution.py:24
  52.0 1.1 copy-start
  63.3 3.9 %copy-start.8 = (f32[27,11]{0,1:T(8,128)S(1)}, f32[27,11]{0,1:T(8,128)}, u32[]{:S(2)}) copy-start(f32[27,11]{0,1:T(8,128)} %constant.118.clone..sunk.2) | copy-start | bytes 3568
  67.9 2.1 copy-start.1
  78.2 2.1 copy-start.1
  88.5 2.1 copy-start.1
  98.7 2.1 copy-start.1
  109.0 2.1 copy-start.1
  119.3 2.1 copy-start.1
  129.6 2.1 copy-start.1
  139.9 2.1 copy-start.1
  149.5 2.3 copy-start.2
  155.0 7.7 %copy-start.3 = (bf16[8,256,128]{1,0,2:T(8,128)(2,1)S(1)}, bf16[8,256,128]{1,0,2:T(8,128)(2,1)}, u32[]{:S(2)}) copy-start(bf16[8,256,128]{1,0,2:T(8,128)(2,1)} %copy.37) | copy-start | bytes 1572868
  155.0 7.7 %copy-start.4 = (bf16[8,256,128]{1,0,2:T(8,128)(2,1)S(1)}, bf16[8,256,128]{1,0,2:T(8,128)(2,1)}, u32[]{:S(2)}) copy-start(bf16[8,256,128]{1,0,2:T(8,128)(2,1)} %copy.38) | copy-start | bytes 1572868
  156.1 19.0 %collective-permute-start.4 = (bf16[8,256,128]{2,0,1:T(8,128)(2,1)}, bf16[8,256,128]{2,0,1:T(8,128)(2,1)}, u32[]{:S(2)}, u32[]{:S(2)}) collective-permute-start(bf16[8,256,128]{2,0,1:T(8,128)(2,1)} %get-tuple-element.296), channel_id=1, source_target_pairs={{0,4},{4,8},{8,12},{1,5},{5,9},{9,13},{2,6},{6,10},{10,14},{3,7},{... | collective-permute-start | bytes 1572872 | tf_op jit(solution)/shard_map/ppermute | solution.py:32
  161.4 16.6 %collective-permute-start.5 = (bf16[8,256,128]{2,0,1:T(8,128)(2,1)}, bf16[8,256,128]{2,0,1:T(8,128)(2,1)}, u32[]{:S(2)}, u32[]{:S(2)}) collective-permute-start(bf16[8,256,128]{2,0,1:T(8,128)(2,1)} %get-tuple-element.297), channel_id=1, source_target_pairs={{4,0},{8,4},{12,8},{5,1},{9,5},{13,9},{6,2},{10,6},{14,10},{7,3},{... | collective-permute-start | bytes 1572872 | tf_op jit(solution)/shard_map/ppermute | solution.py:32
  162.8 4.7 %collective-permute-start.6 = (bf16[2,8,256,7]{2,1,3,0:T(8,128)(2,1)S(1)}, bf16[2,8,256,7]{2,1,3,0:T(8,128)(2,1)S(1)}, u32[]{:S(2)}, u32[]{:S(2)}) collective-permute-start(bf16[2,8,256,7]{2,1,3,0:T(8,128)(2,1)S(1)} %get-tuple-element.300), channel_id=1, source_target_pairs={{0,1},{2,3},{4,5},{6,7},{8,9},{10,11},{12,13},{14,15},{16,17},{18,... | collective-permute-start | bytes 172040 | tf_op jit(solution)/shard_map/ppermute | solution.py:23
  166.1 3.1 %collective-permute-start.7 = (bf16[2,8,256,7]{2,1,3,0:T(8,128)(2,1)S(1)}, bf16[2,8,256,7]{2,1,3,0:T(8,128)(2,1)S(1)}, u32[]{:S(2)}, u32[]{:S(2)}) collective-permute-start(bf16[2,8,256,7]{2,1,3,0:T(8,128)(2,1)S(1)} %get-tuple-element.301), channel_id=1, source_target_pairs={{1,0},{3,2},{5,4},{7,6},{9,8},{11,10},{13,12},{15,14},{17,16},{19,... | collective-permute-start | bytes 172040 | tf_op jit(solution)/shard_map/ppermute | solution.py:24
  262.1 1.0 copy-start.6
Sparse Core Ops, SparseCore 0:
  180.7 20.5 reduce-scatter.1
where the time goes:
time: 273 us; the launch traced here: 270 us
  matrix products  100 us (37%)
  local copies, waits for them, and re-layouts  58.4 us (21%)
  other arithmetic  34.9 us (13%)
  between operations  21.7 us (8%)
  starting transfers between devices  19.9 us (7%)
  loops' own time  19.9 us (7%)
  blocking collectives  10.2 us (4%)
  waiting for transfers between devices  4.78 us (2%)
    dot_general x8, matrix products, matched(): jnp.dot(numer, pcol.astype(jnp.bfloat16), preferred_element_type=jnp.floa...  25.7 us
    dot_general x8, matrix products, convolve(): jnp.einsum('psc,pcd->sd', rows, mats, preferred_element_type=jnp.float32)  22.8 us
    dot_general x8, matrix products, matched(): jnp.dot(denom, (pcol * pcol).astype(jnp.bfloat16), preferred_element_type...  20.9 us
    another operation x1, loops' own time, on_device(): lax.map(matched, (widened[0], widened[1], psf_width.reshape(-1, 2), live))  19.9 us
    dot_general x8, matrix products, convolve(): jnp.einsum('kp,kcd->pcd', mixing, col_tab, precision=lax.Precision.HIGHEST)  16.7 us
    reshape x8, local copies, waits for them, and re-layouts, convolve(): rows = jnp.dot(gr_flat, template, preferred_element_type=jnp.float32).ast...  12.6 us
    dynamic_update_slice x8, other arithmetic, on_device(): lax.map(convolve, (padded, coefficients.reshape(-1, NB), exp_flat, var_fl...  12.5 us
    dot_general x8, matrix products, convolve(): jnp.dot(gr_flat, template, preferred_element_type=jnp.float32)  12.1 us
  transfers between devices with their start and end apart: 9, of which 2 were waited for; matrix products, arithmetic and copies ran while one was open for 33% of the time, Pallas kernels for 0%

commit v1 on v0

v1 whole, which is shorter than its diff:
```python
import functools

import jax
import jax.numpy as jnp
import numpy as np
from jax import lax
from jax.experimental import pallas as pl
from jax.experimental.pallas import tpu as pltpu
from jax.sharding import PartitionSpec as P

HW = 10
PW = 7

sigmas = (0.75, 1.5, 3.0)
degrees = (4, 2, 2)
starts = (0, 5, 8)
profiles = [(group, power) for group in range(3) for power in range(degrees[group] + 1)]

MESH = pl.DeviceIdType.MESH


def scale_of(group, power):
    grid = np.arange(-HW, HW + 1).astype(np.float64)
    base = np.exp(-grid * grid / (2.0 * sigmas[group] ** 2)) * (grid / HW) ** power
    return float(1.0 / np.sqrt(np.sum(base * base)))


def profile_tables(offset):
    spot = offset.astype(jnp.float32)
    inside = jnp.abs(offset) <= HW
    ratio = spot * (1.0 / HW)
    tables = []
    for group in range(3):
        value = jnp.exp(spot * spot * (-0.5 / sigmas[group] ** 2))
        value = jnp.where(inside, value, 0.0)
        for power in range(degrees[group] + 1):
            tables.append(value * scale_of(group, power))
            value = value * ratio
    return tables


def point_table(offset, width):
    rate = -0.5 / (width * width)
    total = 1.0 + 2.0 * sum(jnp.exp(rate * float(u * u)) for u in range(1, PW + 1))
    spot = offset.astype(jnp.float32)
    value = jnp.exp(spot * spot * rate) * (1.0 / total)
    return jnp.where(jnp.abs(offset) <= PW, value, 0.0)


def offsets(rows, cols, shift):
    row = lax.broadcasted_iota(jnp.int32, (rows, cols), 0)
    col = lax.broadcasted_iota(jnp.int32, (rows, cols), 1)
    return col - row + shift


def kernel(
    sizes,
    templates,
    exposures,
    variance,
    coeff,
    psf,
    ids,
    live,
    coadd,
    score,
    win,
    tfull,
    mats,
    gcat,
    gtab,
    cols,
    expo,
    inv,
    wval,
    wfull,
    ifull,
    rden,
    prow,
    qrow,
    pcol,
    qcol,
    psend,
    precv,
    pown,
    xsend,
    xrecv,
    total,
    local_sem,
    var_sem,
    exp_sem,
    out_sem,
    xs_sem,
    xr_sem,
    zs_sem,
    zr_sem,
    ts_sem,
    tr_sem,
    is_sem,
    ir_sem,
    ws_sem,
    wr_sem,
    ps_sem,
    pr_sem,
    ss_sem,
    sr_sem,
):
    Z, X, B = sizes
    owned, S, C = templates.shape[1:]
    slots = ids.shape[2]
    N = ids.shape[1] * slots
    row_patches = X * owned
    z = lax.axis_index("exp")
    x = lax.axis_index("patch")
    b = lax.axis_index("band")

    def column(o):
        return lax.rem(x + o, X)

    def back_column(o):
        return lax.rem(x + X - o, X)

    def other_band(o):
        return lax.rem(b + o, B)

    def back_band(o):
        return lax.rem(b + B - o, B)

    to_exists = (z > 0, z < Z - 1)
    from_exists = (z < Z - 1, z > 0)
    target = (z - 1, z + 1)
    lands = (2, 0)

    def remote(src, dst, send, recv, device):
        return pltpu.make_async_remote_copy(
            src_ref=src,
            dst_ref=dst,
            send_sem=send,
            recv_sem=recv,
            device_id=device,
            device_id_type=MESH,
        )

    barrier = pltpu.get_barrier_semaphore()
    for d in range(2):

        @pl.when(to_exists[d])
        def _():
            pl.semaphore_signal(barrier, inc=1, device_id={"exp": target[d]}, device_id_type=MESH)

    for o in range(1, X):
        pl.semaphore_signal(barrier, inc=1, device_id={"patch": column(o)}, device_id_type=MESH)
    for o in range(1, B):
        pl.semaphore_signal(barrier, inc=1, device_id={"band": other_band(o)}, device_id_type=MESH)

    def var_copy(n):
        return pltpu.make_async_copy(
            variance.at[0, n // slots, lax.rem(n, slots)], inv.at[n], var_sem.at[n]
        )

    def exp_copy(n):
        return pltpu.make_async_copy(
            exposures.at[0, n // slots, lax.rem(n, slots)], expo.at[n], exp_sem.at[n]
        )

    own_copy = pltpu.make_async_copy(
        templates.at[0], win.at[pl.ds(row_patches + x * owned, owned)], local_sem
    )

    def start_local(n, carry):
        var_copy(n).start()
        exp_copy(n).start()
        return carry

    lax.fori_loop(0, N, start_local, 0)
    own_copy.start()
    pl.semaphore_wait(
        barrier,
        (z > 0).astype(jnp.int32) + (z < Z - 1).astype(jnp.int32) + (X - 1) + (B - 1),
    )

    def x_copy(o, i):
        return remote(
            templates.at[0, i],
            win.at[row_patches + x * owned + i],
            xs_sem.at[o, i],
            xr_sem.at[o, i],
            {"patch": back_column(o)},
        )

    def z_copy(d, o, i):
        src = templates.at[0, i] if o == 0 else win.at[row_patches + column(o) * owned + i]
        return remote(
            src,
            win.at[lands[d] * row_patches + column(o) * owned + i],
            zs_sem.at[d, o, i],
            zr_sem.at[d, o, i],
            {"exp": target[d]},
        )

    for i in range(owned):
        for o in range(1, X):
            x_copy(o, i).start()
        for d in range(2):

            @pl.when(to_exists[d])
            def _():
                z_copy(d, 0, i).start()

    for d in range(2):

        @pl.when(jnp.logical_not(from_exists[d]))
        def _():
            for i in range(row_patches):
                win[lands[d] * row_patches + i] = jnp.zeros((S, C), jnp.bfloat16)

    def half_copy(buffer, send, recv, o, n):
        return remote(
            buffer.at[n, :, 0:C],
            buffer.at[n, :, o * C : (o + 1) * C],
            send.at[o, n],
            recv.at[o, n],
            {"band": back_band(o)},
        )

    def invert(n, carry):
        var_copy(n).wait()
        weight = 1.0 / inv[n]
        inv[n] = weight
        ifull[n, :, 0:C] = weight.astype(jnp.bfloat16)
        for o in range(1, B):
            half_copy(ifull, is_sem, ir_sem, o, n).start()
        return carry

    lax.fori_loop(0, N, invert, 0)

    for p, table in enumerate(profile_tables(-offsets(S, S, 0))):
        gcat[:, p * S : (p + 1) * S] = table.astype(jnp.bfloat16)
    shifts = [(b - other_band(o)) * C for o in range(B)]
    for o in range(B):
        for p, table in enumerate(profile_tables(offsets(C, C, shifts[o]))):
            gtab[p, o * C : (o + 1) * C, :] = table

    def forward(o, i):
        x_copy(o, i).wait_recv()
        for d in range(2):

            @pl.when(to_exists[d])
            def _():
                z_copy(d, o, i).start()

    for i in range(owned):
        for o in range(1, X):
            forward(o, i)

    def mix(n, carry):
        e, k = n // slots, lax.rem(n, slots)
        index = 0
        for p, (group, power) in enumerate(profiles):
            value = jnp.zeros((B * C, C), jnp.float32)
            for j in range(degrees[group] + 1 - power):
                value = value + coeff[0, e, k, index] * gtab[starts[group] + j]
                index += 1
            mats[n, :, p * C : (p + 1) * C] = value.astype(jnp.bfloat16)
        return carry

    lax.fori_loop(0, N, mix, 0)

    def spread(n, carry):
        e, k = n // slots, lax.rem(n, slots)
        table = point_table(offsets(S, S, 0), jnp.full((1, S), psf[0, e, k, 0], jnp.float32))
        prow[n] = table.astype(jnp.bfloat16)
        qrow[n] = (table * table).astype(jnp.bfloat16)
        width = jnp.full((1, C), psf[0, e, k, 1], jnp.float32)
        for o in range(B):
            table = point_table(offsets(C, C, shifts[o]), width)
            pcol[n, o * C : (o + 1) * C, :] = table.astype(jnp.bfloat16)
            qcol[n, o * C : (o + 1) * C, :] = (table * table).astype(jnp.bfloat16)
        return carry

    lax.fori_loop(0, N, spread, 0)

    def matched(rows, full, columns):
        middle = jnp.dot(rows, full, preferred_element_type=jnp.float32).astype(jnp.bfloat16)
        return jnp.dot(middle, columns, preferred_element_type=jnp.float32)

    def alive_of(n):
        e, k = n // slots, lax.rem(n, slots)
        return jnp.where(k < live[0, e], 1.0, 0.0).astype(jnp.float32)

    def denominator(n, carry):
        for o in range(1, B):
            half_copy(ifull, is_sem, ir_sem, o, n).wait_recv()
        rden[n] = lax.rsqrt(matched(qrow[n], ifull[n], qcol[n])) * alive_of(n)
        return carry

    lax.fori_loop(0, N, denominator, 0)

    own_copy.wait()
    for d in range(2):

        @pl.when(from_exists[d])
        def _():
            for o in range(X):
                for i in range(owned):
                    z_copy(d, o, i).wait_recv()

    def choose(n, carry):
        exp_copy(n).wait()
        tfull[n, :, 0:C] = win[ids[0, n // slots, lax.rem(n, slots)]]
        for o in range(1, B):
            half_copy(tfull, ts_sem, tr_sem, o, n).start()
        return carry

    lax.fori_loop(0, N, choose, 0)

    count = len(profiles)

    def convolve(pair, carry):
        for h in range(2):
            n = pair * 2 + h
            for o in range(1, B):
                half_copy(tfull, ts_sem, tr_sem, o, n).wait_recv()
            tile = tfull[n]
            for p in range(0, count, 2):
                wide = min(2, count - p)
                part = jnp.dot(
                    tile,
                    mats[n, :, p * C : (p + wide) * C],
                    preferred_element_type=jnp.float32,
                ).astype(jnp.bfloat16)
                for a in range(wide):
                    cols[(p + a) * S : (p + a + 1) * S, h * C : (h + 1) * C] = part[
                        :, a * C : (a + 1) * C
                    ]
        convolved = jnp.dot(gcat[...], cols[...], preferred_element_type=jnp.float32)
        for h in range(2):
            n = pair * 2 + h
            value = (expo[n].astype(jnp.float32) - convolved[:, h * C : (h + 1) * C]) * inv[n]
            wval[n] = value
            wfull[n, :, 0:C] = value.astype(jnp.bfloat16)
            for o in range(1, B):
                half_copy(wfull, ws_sem, wr_sem, o, n).start()
        return carry

    lax.fori_loop(0, N // 2, convolve, 0)

    def partial(patch):
        value = jnp.zeros((S, C), jnp.float32)
        for n in range(N):
            e, k = n // slots, n % slots
            hit = jnp.logical_and(ids[0, e, k] == patch, k < live[0, e])
            value = value + jnp.where(hit, 1.0, 0.0).astype(jnp.float32) * wval[n]
        return value

    def p_copy(d, q, t):
        return remote(
            psend.at[d, q], precv.at[d, q], ps_sem.at[d, t], pr_sem.at[d, t], {"exp": target[d]}
        )

    def patch_of(t):
        return lax.rem(x + 1 + t // owned, X) * owned + lax.rem(t, owned)

    def push(t, carry):
        q = patch_of(t)
        for d, source in ((0, 0), (1, 2)):

            @pl.when(to_exists[d])
            def _():
                psend[d, q] = partial(source * row_patches + q).astype(jnp.bfloat16)
                p_copy(d, q, t).start()

        return carry

    lax.fori_loop(0, row_patches, push, 0)

    def keep(t, carry):
        q = patch_of(t)
        pown[q] = partial(row_patches + q)
        return carry

    lax.fori_loop(0, row_patches, keep, 0)

    def out_copy(n):
        return pltpu.make_async_copy(
            rden.at[n], score.at[0, n // slots, lax.rem(n, slots)], out_sem.at[n]
        )

    def numerator(n, carry):
        for o in range(1, B):
            half_copy(wfull, ws_sem, wr_sem, o, n).wait_recv()
        rden[n] = matched(prow[n], wfull[n], pcol[n]) * rden[n]
        out_copy(n).start()
        return carry

    lax.fori_loop(0, N, numerator, 0)

    def gather_rows(t, q):
        for d in range(2):

            @pl.when(from_exists[d])
            def _():
                p_copy(d, q, t).wait_recv()
                pown[q] = pown[q] + precv[d, q].astype(jnp.float32)

    def s_copy(s, i):
        return remote(
            xsend.at[s, i],
            xrecv.at[s, i],
            ss_sem.at[s, i],
            sr_sem.at[s, i],
            {"patch": column(s + 1)},
        )

    for s in range(X - 1):
        for i in range(owned):
            t = s * owned + i
            q = column(s + 1) * owned + i
            gather_rows(t, q)
            xsend[s, i] = pown[q].astype(jnp.bfloat16)
            s_copy(s, i).start()

    final = []
    for i in range(owned):
        q = x * owned + i
        gather_rows((X - 1) * owned + i, q)
        value = pown[q]
        for s in range(X - 1):
            s_copy(s, i).wait_recv()
            value = value + xrecv[s, i].astype(jnp.float32)
        total[i] = value
        copy = pltpu.make_async_copy(total.at[i], coadd.at[0, i], out_sem.at[N + i])
        copy.start()
        final.append(copy)

    for o in range(1, X):
        for i in range(owned):
            x_copy(o, i).wait_send()
            s_copy(o - 1, i).wait_send()
    for d in range(2):

        @pl.when(to_exists[d])
        def _():
            for o in range(X):
                for i in range(owned):
                    z_copy(d, o, i).wait_send()
            for t in range(row_patches):
                p_copy(d, patch_of(t), t).wait_send()

    def finish(n, carry):
        for o in range(1, B):
            half_copy(ifull, is_sem, ir_sem, o, n).wait_send()
            half_copy(tfull, ts_sem, tr_sem, o, n).wait_send()
            half_copy(wfull, ws_sem, wr_sem, o, n).wait_send()
        out_copy(n).wait()
        return carry

    lax.fori_loop(0, N, finish, 0)
    for copy in final:
        copy.wait()


def on_device(templates, exposures, variance, coefficients, psf_width, patch_ids, live_count):
    owned, S, C = templates.shape[1:]
    Z, X, B = (lax.axis_size(axis) for axis in ("exp", "patch", "band"))
    N = patch_ids.shape[1] * patch_ids.shape[2]
    row = X * owned
    count = len(profiles)
    bf16, f32 = jnp.bfloat16, jnp.float32
    dma = pltpu.SemaphoreType.DMA
    scratch = [
        pltpu.VMEM((3 * row, S, C), bf16),
        pltpu.VMEM((N, S, B * C), bf16),
        pltpu.VMEM((N, B * C, count * C), bf16),
        pltpu.VMEM((S, count * S), bf16),
        pltpu.VMEM((count, B * C, C), f32),
        pltpu.VMEM((count * S, 2 * C), bf16),
        pltpu.VMEM((N, S, C), bf16),
        pltpu.VMEM((N, S, C), f32),
        pltpu.VMEM((N, S, C), f32),
        pltpu.VMEM((N, S, B * C), bf16),
        pltpu.VMEM((N, S, B * C), bf16),
        pltpu.VMEM((N, S, C), f32),
        pltpu.VMEM((N, S, S), bf16),
        pltpu.VMEM((N, S, S), bf16),
        pltpu.VMEM((N, B * C, C), bf16),
        pltpu.VMEM((N, B * C, C), bf16),
        pltpu.VMEM((2, row, S, C), bf16),
        pltpu.VMEM((2, row, S, C), bf16),
        pltpu.VMEM((row, S, C), f32),
        pltpu.VMEM((max(X - 1, 1), owned, S, C), bf16),
        pltpu.VMEM((max(X - 1, 1), owned, S, C), bf16),
        pltpu.VMEM((owned, S, C), f32),
        dma,
        dma((N,)),
        dma((N,)),
        dma((N + owned,)),
        dma((X, owned)),
        dma((X, owned)),
        dma((2, X, owned)),
        dma((2, X, owned)),
        dma((B, N)),
        dma((B, N)),
        dma((B, N)),
        dma((B, N)),
        dma((B, N)),
        dma((B, N)),
        dma((2, row)),
        dma((2, row)),
        dma((max(X - 1, 1), owned)),
        dma((max(X - 1, 1), owned)),
    ]
    any_spec = pl.BlockSpec(memory_space=pl.ANY)
    smem = pl.BlockSpec(memory_space=pltpu.SMEM)
    return pl.pallas_call(
        functools.partial(kernel, (Z, X, B)),
        out_shape=(
            jax.ShapeDtypeStruct(templates.shape, f32),
            jax.ShapeDtypeStruct(exposures.shape, f32),
        ),
        in_specs=[any_spec] * 3 + [smem] * 4,
        out_specs=(any_spec, any_spec),
        scratch_shapes=scratch,
        compiler_params=pltpu.CompilerParams(
            collective_id=0, has_side_effects=True, vmem_limit_bytes=56 * 2**20
        ),
    )(templates, exposures, variance, coefficients, psf_width, patch_ids, live_count)


def solution(mesh):
    in_specs = (
        P(("groups", "exp"), "patch", None, "band"),
        P(("groups", "exp"), "patch", None, None, "band"),
        P(("groups", "exp"), "patch", None, None, "band"),
        P(("groups", "exp"), "patch", None, None),
        P(("groups", "exp"), "patch", None, None),
        P(("groups", "exp"), "patch", None),
        P(("groups", "exp"), "patch"),
    )
    out_specs = (
        P(("groups", "exp"), "patch", None, "band"),
        P(("groups", "exp"), "patch", None, None, "band"),
    )
    return jax.shard_map(
        on_device, mesh=mesh, in_specs=in_specs, out_specs=out_specs, check_vma=False
    )
```

time: 273 us -> 46.4 us (0.17); the launches traced: 270 us -> 46.2 us
  matrix products: 100 us -> 0 us
  local copies, waits for them, and re-layouts: 58.4 us -> 4.29 us
  Pallas kernels: 0 us -> 41.2 us
  other arithmetic: 34.9 us -> 0 us
  between operations: 21.7 us -> 0.65 us
  loops' own time: 19.9 us -> 0 us
  starting transfers between devices: 19.9 us -> 0 us
  blocking collectives: 10.2 us -> 0 us
  waiting for transfers between devices: 4.78 us -> 0 us
    dot_general x41 -> x0, matrix products: 100 us -> none  [the longest x8 25.7 us: matched(): jnp.dot(numer, pcol.astype(jnp.bfloat16), preferred_element_type=jnp.floa...]
    pallas_call x0 -> x1, Pallas kernels: none -> 41.2 us  [on_device(): pl.pallas_call(functools.partial(kernel, (Z, X, B)), out_shape=(jax.Shape...]
    another operation x2 -> x0, loops' own time: 19.9 us -> none  [the longest x1 19.9 us: on_device(): lax.map(matched, (widened[0], widened[1], psf_width.reshape(-1, 2), live))]
    ppermute x8 -> x0, starting transfers between devices: 19.8 us -> none  [the longest x3 9.17 us: with_halo(): before = lax.ppermute(last, axis, up)]
    reshape x10 -> x0, local copies, waits for them, and re-layouts: 13.5 us -> none  [the longest x8 12.6 us: convolve(): rows = jnp.dot(gr_flat, template, preferred_element_type=jnp.float32).ast...]
    dynamic_update_slice x8 -> x0, other arithmetic: 12.5 us -> none  [on_device(): lax.map(convolve, (padded, coefficients.reshape(-1, NB), exp_flat, var_fl...]
    reduce_sum x19 -> x0, other arithmetic: 12.3 us -> none  [the longest x11 7.14 us: profile(): scale = jnp.sqrt(jnp.sum(base * base))]
    another operation x3 -> x0, local copies, waits for them, and re-layouts: 11.3 us -> none  [the longest x1 10.2 us: column_tables(): jnp.stack([profile(offset, sigmas[term[0]], term[2], reach) for term in b...]
  transfers between devices with their start and end apart: 9 -> 0, of which waited for: 2 -> 0; matrix products, arithmetic and copies ran while one was open for 33% -> 0% of each run, Pallas kernels for 0% -> 0%
where the time goes in v1:
time: 46.4 us; the launch traced here: 46.2 us
  Pallas kernels  41.2 us (89%)
  local copies, waits for them, and re-layouts  4.29 us (9%)
  between operations  0.65 us (1%)
    pallas_call x1, Pallas kernels, on_device(): pl.pallas_call(functools.partial(kernel, (Z, X, B)), out_shape=(jax.Shape...  41.2 us
    unnamed x5, local copies, waits for them, and re-layouts  4.29 us

profile of v1, /device:TPU:0, one launch (start us, length us, event | category | flops | bytes accessed | tf_op | source)
XLA Modules:
  0.0 46.2 jit_solution(15639364458564817434)
XLA Ops:
  0.6 1.4 %copy.9.psf = f32[1,2,4,2]{3,2,1,0:T(4,128)} copy(f32[1,2,4,2]{2,3,1,0:T(2,128)} %param.11) | data formatting | bytes 128 | tf_op args[4]
  2.0 41.2 %shard_map.86 = (f32[1,4,256,128]{3,2,1,0:T(8,128)}, f32[1,2,4,256,128]{4,3,2,1,0:T(8,128)}) custom-call(bf16[1,4,256,128]{3,2,1,0:T(8,128)(2,1)} %templates.1, bf16[1,2,4,256,128]{4,3,2,1,0:T(8,128)(2,1)} %exposures.1, f32[1,2,4,256,128]{4,3,2,1,0:T(8,128)} %variance.1, f32[1,2,4,27]{3,2,1,0:T(4,128)} %coeff.1, f32[1,2,4,2]{3,2,1,0:T(4,128)} %copy.9.psf, ...), custom_call_target="tpu_custom_call" | custom-call | tf_op jit(solution)/shard_map/pallas_call | solution.py:515
  43.2 0.0 copy-start
  43.2 2.0 %copy.12 = f32[1,4,256,128]{3,2,1,0:T(8,128)} copy(f32[1,4,256,128]{3,2,1,0:T(8,128)} %get-tuple-element.4) | data formatting | bytes 1048576
  45.2 0.0 copy-done
  45.2 1.0 %copy.13 = f32[1,2,4,256,128]{4,3,2,1,0:T(8,128)} copy(f32[1,2,4,256,128]{4,3,2,1,0:T(8,128)S(1)} %copy-done) | data formatting | bytes 2097152
Async XLA Ops:
  43.2 2.0 %copy-start = (f32[1,2,4,256,128]{4,3,2,1,0:T(8,128)S(1)}, f32[1,2,4,256,128]{4,3,2,1,0:T(8,128)}, u32[]{:S(2)}) copy-start(f32[1,2,4,256,128]{4,3,2,1,0:T(8,128)} %get-tuple-element.5) | copy-start | bytes 3145732

commit v2 on v1

v2 whole, which is shorter than its diff:
```python
import functools

import jax
import jax.numpy as jnp
import numpy as np
from jax import lax
from jax.experimental import pallas as pl
from jax.experimental.pallas import tpu as pltpu
from jax.sharding import PartitionSpec as P

HW = 10
PW = 7

sigmas = (0.75, 1.5, 3.0)
degrees = (4, 2, 2)
starts = (0, 5, 8)
profiles = [(group, power) for group in range(3) for power in range(degrees[group] + 1)]

MESH = pl.DeviceIdType.MESH


def scale_of(group, power):
    grid = np.arange(-HW, HW + 1).astype(np.float64)
    base = np.exp(-grid * grid / (2.0 * sigmas[group] ** 2)) * (grid / HW) ** power
    return float(1.0 / np.sqrt(np.sum(base * base)))


def profile_tables(offset):
    spot = offset.astype(jnp.float32)
    inside = jnp.abs(offset) <= HW
    ratio = spot * (1.0 / HW)
    tables = []
    for group in range(3):
        value = jnp.exp(spot * spot * (-0.5 / sigmas[group] ** 2))
        value = jnp.where(inside, value, 0.0)
        for power in range(degrees[group] + 1):
            tables.append(value * scale_of(group, power))
            value = value * ratio
    return tables


def point_table(offset, width):
    rate = -0.5 / (width * width)
    total = 1.0 + 2.0 * sum(jnp.exp(rate * float(u * u)) for u in range(1, PW + 1))
    spot = offset.astype(jnp.float32)
    value = jnp.exp(spot * spot * rate) * (1.0 / total)
    return jnp.where(jnp.abs(offset) <= PW, value, 0.0)


def offsets(rows, cols, shift):
    row = lax.broadcasted_iota(jnp.int32, (rows, cols), 0)
    col = lax.broadcasted_iota(jnp.int32, (rows, cols), 1)
    return col - row + shift


def kernel(
    sizes,
    templates,
    exposures,
    variance,
    coeff,
    psf,
    ids,
    live,
    coadd,
    score,
    win0,
    win1,
    tfull,
    mats,
    gcat,
    gtab,
    cols,
    expo,
    inv,
    wval,
    wfull,
    ifull,
    rden,
    prow,
    qrow,
    pcol,
    qcol,
    psend,
    precv,
    pown,
    xsend,
    xrecv,
    total,
    local_sem,
    var_sem,
    exp_sem,
    out_sem,
    xs_sem,
    xr_sem,
    zs_sem,
    zr_sem,
    ts_sem,
    tr_sem,
    is_sem,
    ir_sem,
    ws_sem,
    wr_sem,
    ps_sem,
    pr_sem,
    ss_sem,
    sr_sem,
):
    Z, X, B = sizes
    owned, S, C = templates.shape[1:]
    slots = ids.shape[2]
    N = ids.shape[1] * slots
    row_patches = X * owned
    z = lax.axis_index("exp")
    x = lax.axis_index("patch")
    b = lax.axis_index("band")

    def column(o):
        return lax.rem(x + o, X)

    def back_column(o):
        return lax.rem(x + X - o, X)

    def other_band(o):
        return lax.rem(b + o, B)

    def back_band(o):
        return lax.rem(b + B - o, B)

    to_exists = (z > 0, z < Z - 1)
    from_exists = (z < Z - 1, z > 0)
    target = (z - 1, z + 1)
    lands = (2, 0)

    def remote(src, dst, send, recv, device):
        return pltpu.make_async_remote_copy(
            src_ref=src,
            dst_ref=dst,
            send_sem=send,
            recv_sem=recv,
            device_id=device,
            device_id_type=MESH,
        )

    barrier = pltpu.get_barrier_semaphore()
    for d in range(2):

        @pl.when(to_exists[d])
        def _():
            pl.semaphore_signal(barrier, inc=1, device_id={"exp": target[d]}, device_id_type=MESH)

    for o in range(1, X):
        pl.semaphore_signal(barrier, inc=1, device_id={"patch": column(o)}, device_id_type=MESH)
    for o in range(1, B):
        pl.semaphore_signal(barrier, inc=1, device_id={"band": other_band(o)}, device_id_type=MESH)

    H = S // 2
    win = (win0, win1)
    gs = max(owned // 2, 1)
    groups = owned // gs
    bounds = ((0, H - 16), (H - 16, S))

    def var_copy(n):
        return pltpu.make_async_copy(
            variance.at[0, n // slots, lax.rem(n, slots)], inv.at[n], var_sem.at[n]
        )

    def exp_copy(n):
        return pltpu.make_async_copy(
            exposures.at[0, n // slots, lax.rem(n, slots)], expo.at[n], exp_sem.at[n]
        )

    def own_copy(h):
        return pltpu.make_async_copy(
            templates.at[0, :, pl.ds(h * H, H)],
            win[h].at[pl.ds(row_patches + x * owned, owned)],
            local_sem.at[h],
        )

    def start_local(n, carry):
        var_copy(n).start()
        return carry

    lax.fori_loop(0, N, start_local, 0)
    pl.semaphore_wait(
        barrier,
        (z > 0).astype(jnp.int32) + (z < Z - 1).astype(jnp.int32) + (X - 1) + (B - 1),
    )

    def block(h, i):
        return templates.at[0, pl.ds(i * gs, gs), pl.ds(h * H, H)]

    def place(h, row, o, i):
        return win[h].at[pl.ds(row * row_patches + column(o) * owned + i * gs, gs)]

    def x_copy(h, o, i):
        return remote(
            block(h, i),
            place(h, 1, 0, i),
            xs_sem.at[h, o, i],
            xr_sem.at[h, o, i],
            {"patch": back_column(o)},
        )

    def z_copy(h, d, o, i):
        return remote(
            block(h, i) if o == 0 else place(h, 1, o, i),
            place(h, lands[d], o, i),
            zs_sem.at[h, d, o, i],
            zr_sem.at[h, d, o, i],
            {"exp": target[d]},
        )

    def launch(h):
        for i in range(groups):
            for o in range(1, X):
                x_copy(h, o, i).start()
            for d in range(2):

                @pl.when(to_exists[d])
                def _():
                    z_copy(h, d, 0, i).start()

    def forward(h):
        for i in range(groups):
            for o in range(1, X):
                x_copy(h, o, i).wait_recv()
                for d in range(2):

                    @pl.when(to_exists[d])
                    def _():
                        z_copy(h, d, o, i).start()

    def half_copy(buffer, send, recv, o, n):
        return remote(
            buffer.at[n, :, 0:C],
            buffer.at[n, :, o * C : (o + 1) * C],
            send.at[o, n],
            recv.at[o, n],
            {"band": back_band(o)},
        )

    def invert(n, carry):
        var_copy(n).wait()
        weight = 1.0 / inv[n]
        inv[n] = weight
        ifull[n, :, 0:C] = weight.astype(jnp.bfloat16)
        for o in range(1, B):
            half_copy(ifull, is_sem, ir_sem, o, n).start()
        return carry

    launch(0)

    def start_exposure(n, carry):
        exp_copy(n).start()
        return carry

    lax.fori_loop(0, N, start_exposure, 0)
    for h in range(2):
        own_copy(h).start()
    lax.fori_loop(0, N // 2, invert, 0)
    forward(0)
    launch(1)
    lax.fori_loop(N // 2, N, invert, 0)

    count = len(profiles)
    gcat[...] = jnp.zeros((S, 2 * count * H), jnp.bfloat16)
    for p, table in enumerate(profile_tables(-offsets(H, H, 0))):
        table = table.astype(jnp.bfloat16)
        gcat[0:H, p * H : (p + 1) * H] = table
        gcat[H:S, (count + p) * H : (count + p + 1) * H] = table
    for p, table in enumerate(profile_tables(-offsets(16, H, -H))):
        gcat[H : H + 16, p * H : (p + 1) * H] = table.astype(jnp.bfloat16)
    for p, table in enumerate(profile_tables(-offsets(16, H, 16))):
        gcat[H - 16 : H, (count + p) * H : (count + p + 1) * H] = table.astype(jnp.bfloat16)
    shifts = [(b - other_band(o)) * C for o in range(B)]
    for p, table in enumerate(profile_tables(offsets(C, C, 0))):
        gtab[p, 0:C, :] = table
    for o in range(1, B):
        start = C + (o - 1) * 32
        for p, table in enumerate(profile_tables(offsets(16, C, shifts[o]))):
            gtab[p, start : start + 16, :] = table
        for p, table in enumerate(profile_tables(offsets(16, C, shifts[o] - C + 16))):
            gtab[p, start + 16 : start + 32, :] = table

    def mix(n, carry):
        e, k = n // slots, lax.rem(n, slots)
        if B > 1:
            mats[n, C : B * C, :] = jnp.zeros(((B - 1) * C, count * C), jnp.bfloat16)
        index = 0
        for p, (group, power) in enumerate(profiles):
            value = coeff[0, e, k, index] * gtab[starts[group]]
            index += 1
            for j in range(1, degrees[group] + 1 - power):
                value = value + coeff[0, e, k, index] * gtab[starts[group] + j]
                index += 1
            value = value.astype(jnp.bfloat16)
            lanes = slice(p * C, (p + 1) * C)
            mats[n, 0:C, lanes] = value[0:C]
            for o in range(1, B):
                start = C + (o - 1) * 32
                mats[n, o * C : o * C + 16, lanes] = value[start : start + 16]
                mats[n, (o + 1) * C - 16 : (o + 1) * C, lanes] = value[start + 16 : start + 32]
        return carry

    lax.fori_loop(0, N, mix, 0)
    forward(1)

    for d in range(2):

        @pl.when(jnp.logical_not(from_exists[d]))
        def _():
            for h in range(2):

                def clear(i, carry):
                    win[h][lands[d] * row_patches + i] = jnp.zeros((H, C), jnp.bfloat16)
                    return carry

                lax.fori_loop(0, row_patches, clear, 0)

    def spread(n, carry):
        e, k = n // slots, lax.rem(n, slots)

        def put(low, square, rows, lanes, table):
            low[n, rows, lanes] = table.astype(jnp.bfloat16)
            square[n, rows, lanes] = (table * table).astype(jnp.bfloat16)

        width = jnp.full((1, H), psf[0, e, 0, k], jnp.float32)
        prow[n] = jnp.zeros((S, S), jnp.bfloat16)
        qrow[n] = jnp.zeros((S, S), jnp.bfloat16)
        table = point_table(offsets(H, H, 0), width)
        put(prow, qrow, slice(0, H), slice(0, H), table)
        put(prow, qrow, slice(H, S), slice(H, S), table)
        put(prow, qrow, slice(H, H + 16), slice(0, H), point_table(offsets(16, H, -H), width))
        put(prow, qrow, slice(H - 16, H), slice(H, S), point_table(offsets(16, H, 16), width))
        width = jnp.full((1, C), psf[0, e, 1, k], jnp.float32)
        pcol[n] = jnp.zeros((B * C, C), jnp.bfloat16)
        qcol[n] = jnp.zeros((B * C, C), jnp.bfloat16)
        lanes = slice(0, C)
        put(pcol, qcol, slice(0, C), lanes, point_table(offsets(C, C, 0), width))
        for o in range(1, B):
            first, last = o * C, (o + 1) * C
            table = point_table(offsets(16, C, shifts[o]), width)
            put(pcol, qcol, slice(first, first + 16), lanes, table)
            table = point_table(offsets(16, C, shifts[o] - C + 16), width)
            put(pcol, qcol, slice(last - 16, last), lanes, table)
        return carry

    def alive_of(n):
        e, k = n // slots, lax.rem(n, slots)
        return jnp.where(k < live[0, e], 1.0, 0.0).astype(jnp.float32)

    def matched(chains):
        middle = [
            jnp.dot(rows, full, preferred_element_type=jnp.float32).astype(jnp.bfloat16)
            for rows, full, _ in chains
        ]
        return [
            jnp.dot(part, chain[2], preferred_element_type=jnp.float32)
            for part, chain in zip(middle, chains)
        ]

    def denominator(pair, carry):
        tiles = (pair * 2, pair * 2 + 1)
        for n in tiles:
            for o in range(1, B):
                half_copy(ifull, is_sem, ir_sem, o, n).wait_recv()
        results = matched([(qrow[n], ifull[n], qcol[n]) for n in tiles])
        for n, result in zip(tiles, results):
            rden[n] = lax.rsqrt(result) * alive_of(n)
        return carry

    def arrive(h):
        own_copy(h).wait()
        for d in range(2):

            @pl.when(from_exists[d])
            def _():
                for o in range(X):
                    for i in range(groups):
                        z_copy(h, d, o, i).wait_recv()

    def tile_copy(h, o, n):
        return remote(
            tfull.at[h, n, :, 0:C],
            tfull.at[h, n, :, o * C : (o + 1) * C],
            ts_sem.at[h, o, n],
            tr_sem.at[h, o, n],
            {"band": back_band(o)},
        )

    def middle(h):
        first, last = bounds[h]
        depth = (h + 1) * count * H

        def choose(n, carry):
            tfull[h, n, :, 0:C] = win[h][ids[0, n // slots, lax.rem(n, slots)]]
            for o in range(1, B):
                tile_copy(h, o, n).start()
            return carry

        lax.fori_loop(0, N, choose, 0)

        def convolve(pair, carry):
            for a in range(2):
                n = pair * 2 + a
                if h == 0:
                    exp_copy(n).wait()
                for o in range(1, B):
                    tile_copy(h, o, n).wait_recv()
                tile = tfull[h, n]
                for p in range(0, count, 2):
                    wide = min(2, count - p)
                    part = jnp.dot(
                        tile,
                        mats[n, :, p * C : (p + wide) * C],
                        preferred_element_type=jnp.float32,
                    ).astype(jnp.bfloat16)
                    for v in range(wide):
                        row = (h * count + p + v) * H
                        cols[pair, row : row + H, a * C : (a + 1) * C] = part[
                            :, v * C : (v + 1) * C
                        ]
            convolved = jnp.dot(
                gcat[first:last, 0:depth],
                cols[pair, 0:depth, :],
                preferred_element_type=jnp.float32,
            )
            for a in range(2):
                n = pair * 2 + a
                value = expo[n, first:last, :].astype(jnp.float32)
                value = (value - convolved[:, a * C : (a + 1) * C]) * inv[n, first:last, :]
                wval[n, first:last, :] = value
                wfull[n, first:last, 0:C] = value.astype(jnp.bfloat16)
                if h == 1:
                    for o in range(1, B):
                        half_copy(wfull, ws_sem, wr_sem, o, n).start()
            return carry

        lax.fori_loop(0, N // 2, convolve, 0)

    def partial(h, patch):
        first, last = bounds[h]
        value = jnp.zeros((last - first, C), jnp.float32)
        for n in range(N):
            e, k = n // slots, n % slots
            hit = jnp.logical_and(ids[0, e, k] == patch, k < live[0, e])
            factor = jnp.where(hit, 1.0, 0.0).astype(jnp.float32)
            value = value + factor * wval[n, first:last, :]
        return value

    def p_copy(h, d, q, t):
        first, last = bounds[h]
        rows = pl.ds(first, last - first)
        return remote(
            psend.at[d, q, rows],
            precv.at[d, q, rows],
            ps_sem.at[h, d, t],
            pr_sem.at[h, d, t],
            {"exp": target[d]},
        )

    def patch_of(t):
        return lax.rem(x + 1 + t // owned, X) * owned + lax.rem(t, owned)

    def push(h):
        first, last = bounds[h]

        def step(t, carry):
            q = patch_of(t)
            for d, source in ((0, 0), (1, 2)):

                @pl.when(to_exists[d])
                def _():
                    value = partial(h, source * row_patches + q)
                    psend[d, q, first:last, :] = value.astype(jnp.bfloat16)
                    p_copy(h, d, q, t).start()

            return carry

        lax.fori_loop(0, row_patches, step, 0)

    def keep(h):
        first, last = bounds[h]

        def step(q, carry):
            pown[q, first:last, :] = partial(h, row_patches + q)
            return carry

        lax.fori_loop(0, row_patches, step, 0)

    def out_copy(n):
        return pltpu.make_async_copy(
            rden.at[n], score.at[0, n // slots, lax.rem(n, slots)], out_sem.at[n]
        )

    def numerator(pair, carry):
        tiles = (pair * 2, pair * 2 + 1)
        for n in tiles:
            for o in range(1, B):
                half_copy(wfull, ws_sem, wr_sem, o, n).wait_recv()
        results = matched([(prow[n], wfull[n], pcol[n]) for n in tiles])
        for n, result in zip(tiles, results):
            rden[n] = result * rden[n]
            out_copy(n).start()
        return carry

    def gather_rows(h, t, q):
        first, last = bounds[h]
        for d in range(2):

            @pl.when(from_exists[d])
            def _():
                p_copy(h, d, q, t).wait_recv()
                pown[q, first:last, :] += precv[d, q, first:last, :].astype(jnp.float32)

    def s_copy(h, s, i):
        first, last = bounds[h]
        rows = pl.ds(first, last - first)
        return remote(
            xsend.at[s, i, rows],
            xrecv.at[s, i, rows],
            ss_sem.at[h, s, i],
            sr_sem.at[h, s, i],
            {"patch": column(s + 1)},
        )

    def pass_on(h):
        first, last = bounds[h]
        for s in range(X - 1):
            for i in range(owned):
                q = column(s + 1) * owned + i
                gather_rows(h, s * owned + i, q)
                xsend[s, i, first:last, :] = pown[q, first:last, :].astype(jnp.bfloat16)
                s_copy(h, s, i).start()

    def final_copy(h, i):
        first, last = bounds[h]
        rows = pl.ds(first, last - first)
        return pltpu.make_async_copy(
            total.at[i, rows], coadd.at[0, i, rows], out_sem.at[N + h * owned + i]
        )

    def finish_sums(h):
        first, last = bounds[h]
        for i in range(owned):
            q = x * owned + i
            gather_rows(h, (X - 1) * owned + i, q)
            value = pown[q, first:last, :]
            for s in range(X - 1):
                s_copy(h, s, i).wait_recv()
                value = value + xrecv[s, i, first:last, :].astype(jnp.float32)
            total[i, first:last, :] = value
            final_copy(h, i).start()

    arrive(0)
    middle(0)
    push(0)
    lax.fori_loop(0, N, spread, 0)
    arrive(1)
    middle(1)
    push(1)
    keep(0)
    pass_on(0)
    keep(1)
    lax.fori_loop(0, N // 2, denominator, 0)
    pass_on(1)
    finish_sums(0)
    lax.fori_loop(0, N // 2, numerator, 0)
    finish_sums(1)

    for h in range(2):
        for o in range(1, X):
            for i in range(groups):
                x_copy(h, o, i).wait_send()
            for i in range(owned):
                s_copy(h, o - 1, i).wait_send()
        for i in range(owned):
            final_copy(h, i).wait()
        for d in range(2):

            @pl.when(to_exists[d])
            def _():
                for o in range(X):
                    for i in range(groups):
                        z_copy(h, d, o, i).wait_send()

                def sent(t, carry):
                    p_copy(h, d, patch_of(t), t).wait_send()
                    return carry

                lax.fori_loop(0, row_patches, sent, 0)

    def finish(n, carry):
        for o in range(1, B):
            half_copy(ifull, is_sem, ir_sem, o, n).wait_send()
            half_copy(wfull, ws_sem, wr_sem, o, n).wait_send()
            for h in range(2):
                tile_copy(h, o, n).wait_send()
        out_copy(n).wait()
        return carry

    lax.fori_loop(0, N, finish, 0)


def on_device(templates, exposures, variance, coefficients, psf_width, patch_ids, live_count):
    owned, S, C = templates.shape[1:]
    Z, X, B = (lax.axis_size(axis) for axis in ("exp", "patch", "band"))
    N = patch_ids.shape[1] * patch_ids.shape[2]
    row = X * owned
    count = len(profiles)
    bf16, f32 = jnp.bfloat16, jnp.float32
    dma = pltpu.SemaphoreType.DMA
    scratch = [
        pltpu.VMEM((3 * row, S // 2, C), bf16),
        pltpu.VMEM((3 * row, S // 2, C), bf16),
        pltpu.VMEM((2, N, S // 2, B * C), bf16),
        pltpu.VMEM((N, B * C, count * C), bf16),
        pltpu.VMEM((S, count * S), bf16),
        pltpu.VMEM((count, C + 32 * (B - 1), C), f32),
        pltpu.VMEM((N // 2, count * S, 2 * C), bf16),
        pltpu.VMEM((N, S, C), bf16),
        pltpu.VMEM((N, S, C), f32),
        pltpu.VMEM((N, S, C), f32),
        pltpu.VMEM((N, S, B * C), bf16),
        pltpu.VMEM((N, S, B * C), bf16),
        pltpu.VMEM((N, S, C), f32),
        pltpu.VMEM((N, S, S), bf16),
        pltpu.VMEM((N, S, S), bf16),
        pltpu.VMEM((N, B * C, C), bf16),
        pltpu.VMEM((N, B * C, C), bf16),
        pltpu.VMEM((2, row, S, C), bf16),
        pltpu.VMEM((2, row, S, C), bf16),
        pltpu.VMEM((row, S, C), f32),
        pltpu.VMEM((max(X - 1, 1), owned, S, C), bf16),
        pltpu.VMEM((max(X - 1, 1), owned, S, C), bf16),
        pltpu.VMEM((owned, S, C), f32),
        dma((2,)),
        dma((N,)),
        dma((N,)),
        dma((N + 2 * owned,)),
        dma((2, X, owned)),
        dma((2, X, owned)),
        dma((2, 2, X, owned)),
        dma((2, 2, X, owned)),
        dma((2, B, N)),
        dma((2, B, N)),
        dma((B, N)),
        dma((B, N)),
        dma((B, N)),
        dma((B, N)),
        dma((2, 2, row)),
        dma((2, 2, row)),
        dma((2, max(X - 1, 1), owned)),
        dma((2, max(X - 1, 1), owned)),
    ]
    any_spec = pl.BlockSpec(memory_space=pl.ANY)
    smem = pl.BlockSpec(memory_space=pltpu.SMEM)
    return pl.pallas_call(
        functools.partial(kernel, (Z, X, B)),
        out_shape=(
            jax.ShapeDtypeStruct(templates.shape, f32),
            jax.ShapeDtypeStruct(exposures.shape, f32),
        ),
        in_specs=[any_spec] * 3 + [smem] * 4,
        out_specs=(any_spec, any_spec),
        scratch_shapes=scratch,
        compiler_params=pltpu.CompilerParams(
            collective_id=0, has_side_effects=True, vmem_limit_bytes=56 * 2**20
        ),
    )(
        templates,
        exposures,
        variance,
        coefficients,
        jnp.swapaxes(psf_width, 2, 3),
        patch_ids,
        live_count,
    )


def solution(mesh):
    in_specs = (
        P(("groups", "exp"), "patch", None, "band"),
        P(("groups", "exp"), "patch", None, None, "band"),
        P(("groups", "exp"), "patch", None, None, "band"),
        P(("groups", "exp"), "patch", None, None),
        P(("groups", "exp"), "patch", None, None),
        P(("groups", "exp"), "patch", None),
        P(("groups", "exp"), "patch"),
    )
    out_specs = (
        P(("groups", "exp"), "patch", None, "band"),
        P(("groups", "exp"), "patch", None, None, "band"),
    )
    return jax.shard_map(
        on_device, mesh=mesh, in_specs=in_specs, out_specs=out_specs, check_vma=False
    )
```

time: 46.4 us -> 40.7 us (0.88)
  Pallas kernels: 41.2 us -> 36.9 us
  local copies, waits for them, and re-layouts: 4.29 us -> 2.93 us
    pallas_call x1, Pallas kernels: 41.2 us -> 36.9 us  [on_device(): pl.pallas_call(functools.partial(kernel, (Z, X, B)), out_shape=(jax.Shape...]
    unnamed x5 -> x4, local copies, waits for them, and re-layouts: 4.29 us -> 2.93 us
where the time goes in v2:
time: 40.7 us; the launch traced here: 40.5 us
  Pallas kernels  36.9 us (91%)
  local copies, waits for them, and re-layouts  2.93 us (7%)
  between operations  0.65 us (2%)
    pallas_call x1, Pallas kernels, on_device(): pl.pallas_call(functools.partial(kernel, (Z, X, B)), out_shape=(jax.Shape...  36.9 us
    unnamed x4, local copies, waits for them, and re-layouts  2.93 us

profile of v2, /device:TPU:0, one launch (start us, length us, event | category | flops | bytes accessed | tf_op | source)
XLA Modules:
  0.0 40.5 jit_solution(16529727050690481266)
XLA Ops:
  0.6 36.9 %shard_map.86 = (f32[1,4,256,128]{3,2,1,0:T(8,128)}, f32[1,2,4,256,128]{4,3,2,1,0:T(8,128)}) custom-call(bf16[1,4,256,128]{3,2,1,0:T(8,128)(2,1)} %templates.1, bf16[1,2,4,256,128]{4,3,2,1,0:T(8,128)(2,1)} %exposures.1, f32[1,2,4,256,128]{4,3,2,1,0:T(8,128)} %variance.1, f32[1,2,4,27]{3,2,1,0:T(4,128)} %coeff.1, f32[1,2,2,4]{3,2,1,0:T(2,128)} %bitcast.1, ...), custom_call_target="tpu_custom_call" | custom-call | tf_op jit(solution)/shard_map/pallas_call | solution.py:659
  37.5 0.0 copy-start
  37.5 2.0 %copy.11 = f32[1,4,256,128]{3,2,1,0:T(8,128)} copy(f32[1,4,256,128]{3,2,1,0:T(8,128)} %get-tuple-element.4) | data formatting | bytes 1048576
  39.5 0.0 copy-done
  39.5 1.0 %copy.12 = f32[1,2,4,256,128]{4,3,2,1,0:T(8,128)} copy(f32[1,2,4,256,128]{4,3,2,1,0:T(8,128)S(1)} %copy-done) | data formatting | bytes 2097152
Async XLA Ops:
  37.5 2.0 %copy-start = (f32[1,2,4,256,128]{4,3,2,1,0:T(8,128)S(1)}, f32[1,2,4,256,128]{4,3,2,1,0:T(8,128)}, u32[]{:S(2)}) copy-start(f32[1,2,4,256,128]{4,3,2,1,0:T(8,128)} %get-tuple-element.5) | copy-start | bytes 3145732

commit v3 on v2

--- a/solution.py
+++ b/solution.py
@@ -86,11 +86,9 @@
     pown,
     xsend,
     xrecv,
-    total,
     local_sem,
     var_sem,
     exp_sem,
-    out_sem,
     xs_sem,
     xr_sem,
     zs_sem,
@@ -439,15 +437,23 @@
 
         lax.fori_loop(0, N // 2, convolve, 0)
 
-    def partial(h, patch):
+    def partials(h, q, rows):
         first, last = bounds[h]
-        value = jnp.zeros((last - first, C), jnp.float32)
-        for n in range(N):
-            e, k = n // slots, n % slots
-            hit = jnp.logical_and(ids[0, e, k] == patch, k < live[0, e])
-            factor = jnp.where(hit, 1.0, 0.0).astype(jnp.float32)
-            value = value + factor * wval[n, first:last, :]
-        return value
+        factors = []
+        for row in rows:
+            hits = []
+            for n in range(N):
+                e, k = n // slots, n % slots
+                hit = jnp.logical_and(ids[0, e, k] == row * row_patches + q, k < live[0, e])
+                hits.append(jnp.where(hit, 1.0, 0.0).astype(jnp.float32))
+            factors.append(hits)
+        step = 16
+        for start in range(first, last, step):
+            values = [jnp.zeros((step, C), jnp.float32) for _ in rows]
+            for n in range(N):
+                tile = wval[n, start : start + step, :]
+                values = [value + hits[n] * tile for value, hits in zip(values, factors)]
+            yield slice(start, start + step), values
 
     def p_copy(h, d, q, t):
         first, last = bounds[h]
@@ -464,35 +470,21 @@
         return lax.rem(x + 1 + t // owned, X) * owned + lax.rem(t, owned)
 
     def push(h):
-        first, last = bounds[h]
-
         def step(t, carry):
             q = patch_of(t)
-            for d, source in ((0, 0), (1, 2)):
+            for rows, (up, own, down) in partials(h, q, (0, 1, 2)):
+                psend[0, q, rows, :] = up.astype(jnp.bfloat16)
+                psend[1, q, rows, :] = down.astype(jnp.bfloat16)
+                pown[q, rows, :] = own
+            for d in range(2):
 
                 @pl.when(to_exists[d])
                 def _():
-                    value = partial(h, source * row_patches + q)
-                    psend[d, q, first:last, :] = value.astype(jnp.bfloat16)
                     p_copy(h, d, q, t).start()
 
             return carry
 
         lax.fori_loop(0, row_patches, step, 0)
-
-    def keep(h):
-        first, last = bounds[h]
-
-        def step(q, carry):
-            pown[q, first:last, :] = partial(h, row_patches + q)
-            return carry
-
-        lax.fori_loop(0, row_patches, step, 0)
-
-    def out_copy(n):
-        return pltpu.make_async_copy(
-            rden.at[n], score.at[0, n // slots, lax.rem(n, slots)], out_sem.at[n]
-        )
 
     def numerator(pair, carry):
         tiles = (pair * 2, pair * 2 + 1)
@@ -501,8 +493,7 @@
                 half_copy(wfull, ws_sem, wr_sem, o, n).wait_recv()
         results = matched([(prow[n], wfull[n], pcol[n]) for n in tiles])
         for n, result in zip(tiles, results):
-            rden[n] = result * rden[n]
-            out_copy(n).start()
+            score[0, n // slots, lax.rem(n, slots)] = result * rden[n]
         return carry
 
     def gather_rows(h, t, q):
@@ -534,13 +525,6 @@
                 xsend[s, i, first:last, :] = pown[q, first:last, :].astype(jnp.bfloat16)
                 s_copy(h, s, i).start()
 
-    def final_copy(h, i):
-        first, last = bounds[h]
-        rows = pl.ds(first, last - first)
-        return pltpu.make_async_copy(
-            total.at[i, rows], coadd.at[0, i, rows], out_sem.at[N + h * owned + i]
-        )
-
     def finish_sums(h):
         first, last = bounds[h]
         for i in range(owned):
@@ -550,8 +534,7 @@
             for s in range(X - 1):
                 s_copy(h, s, i).wait_recv()
                 value = value + xrecv[s, i, first:last, :].astype(jnp.float32)
-            total[i, first:last, :] = value
-            final_copy(h, i).start()
+            coadd[0, i, first:last, :] = value
 
     arrive(0)
     middle(0)
@@ -560,9 +543,7 @@
     arrive(1)
     middle(1)
     push(1)
-    keep(0)
     pass_on(0)
-    keep(1)
     lax.fori_loop(0, N // 2, denominator, 0)
     pass_on(1)
     finish_sums(0)
@@ -575,8 +556,6 @@
                 x_copy(h, o, i).wait_send()
             for i in range(owned):
                 s_copy(h, o - 1, i).wait_send()
-        for i in range(owned):
-            final_copy(h, i).wait()
         for d in range(2):
 
             @pl.when(to_exists[d])
@@ -597,7 +576,6 @@
             half_copy(wfull, ws_sem, wr_sem, o, n).wait_send()
             for h in range(2):
                 tile_copy(h, o, n).wait_send()
-        out_copy(n).wait()
         return carry
 
     lax.fori_loop(0, N, finish, 0)
@@ -634,11 +612,9 @@
         pltpu.VMEM((row, S, C), f32),
         pltpu.VMEM((max(X - 1, 1), owned, S, C), bf16),
         pltpu.VMEM((max(X - 1, 1), owned, S, C), bf16),
-        pltpu.VMEM((owned, S, C), f32),
         dma((2,)),
         dma((N,)),
         dma((N,)),
-        dma((N + 2 * owned,)),
         dma((2, X, owned)),
         dma((2, X, owned)),
         dma((2, 2, X, owned)),
@@ -655,15 +631,16 @@
         dma((2, max(X - 1, 1), owned)),
     ]
     any_spec = pl.BlockSpec(memory_space=pl.ANY)
+    vmem = pl.BlockSpec(memory_space=pltpu.VMEM)
     smem = pl.BlockSpec(memory_space=pltpu.SMEM)
     return pl.pallas_call(
         functools.partial(kernel, (Z, X, B)),
         out_shape=(
-            jax.ShapeDtypeStruct(templates.shape, f32),
-            jax.ShapeDtypeStruct(exposures.shape, f32),
+            pltpu.VMEM(templates.shape, f32),
+            pltpu.VMEM(exposures.shape, f32),
         ),
         in_specs=[any_spec] * 3 + [smem] * 4,
-        out_specs=(any_spec, any_spec),
+        out_specs=(vmem, vmem),
         scratch_shapes=scratch,
         compiler_params=pltpu.CompilerParams(
             collective_id=0, has_side_effects=True, vmem_limit_bytes=56 * 2**20

time: 40.7 us -> 39 us (0.958)
  local copies, waits for them, and re-layouts: 2.93 us -> 1.77 us
    unnamed x4 -> x2, local copies, waits for them, and re-layouts: 2.93 us -> 1.77 us
    pallas_call x1, Pallas kernels: 36.9 us -> 36.5 us  [on_device(): pl.pallas_call(functools.partial(kernel, (Z, X, B)), out_shape=(pltpu.VME...]
where the time goes in v3:
time: 39 us; the launch traced here: 38.9 us
  Pallas kernels  36.5 us (94%)
  local copies, waits for them, and re-layouts  1.77 us (5%)
  between operations  0.64 us (2%)
    pallas_call x1, Pallas kernels, on_device(): pl.pallas_call(functools.partial(kernel, (Z, X, B)), out_shape=(pltpu.VME...  36.5 us
    unnamed x2, local copies, waits for them, and re-layouts  1.77 us

profile of v3, /device:TPU:0, one launch (start us, length us, event | category | flops | bytes accessed | tf_op | source)
XLA Modules:
  0.0 38.9 jit_solution(7282574850388840214)
XLA Ops:
  0.6 36.5 %shard_map.86 = (f32[1,4,256,128]{3,2,1,0:T(8,128)S(1)}, f32[1,2,4,256,128]{4,3,2,1,0:T(8,128)S(1)}) custom-call(bf16[1,4,256,128]{3,2,1,0:T(8,128)(2,1)} %templates.1, bf16[1,2,4,256,128]{4,3,2,1,0:T(8,128)(2,1)} %exposures.1, f32[1,2,4,256,128]{4,3,2,1,0:T(8,128)} %variance.1, f32[1,2,4,27]{3,2,1,0:T(4,128)} %coeff.1, f32[1,2,2,4]{3,2,1,0:T(2,128)} %bitcast.1, ...), custom_call_target="tpu_custom_call" | custom-call | tf_op jit(solution)/shard_map/pallas_call | solution.py:636
  37.1 0.8 %copy.11 = f32[1,4,256,128]{3,2,1,0:T(8,128)} copy(f32[1,4,256,128]{3,2,1,0:T(8,128)S(1)} %get-tuple-element.2) | data formatting | bytes 1048576
  37.9 1.0 %copy.12 = f32[1,2,4,256,128]{4,3,2,1,0:T(8,128)} copy(f32[1,2,4,256,128]{4,3,2,1,0:T(8,128)S(1)} %get-tuple-element.3) | data formatting | bytes 2097152

commit v4 on v3

--- a/solution.py
+++ b/solution.py
@@ -10,6 +10,7 @@
 
 HW = 10
 PW = 7
+PARTS = 4
 
 sigmas = (0.75, 1.5, 3.0)
 degrees = (4, 2, 2)
@@ -66,6 +67,8 @@
     score,
     win0,
     win1,
+    win2,
+    win3,
     tfull,
     mats,
     gcat,
@@ -152,11 +155,11 @@
     for o in range(1, B):
         pl.semaphore_signal(barrier, inc=1, device_id={"band": other_band(o)}, device_id_type=MESH)
 
-    H = S // 2
-    win = (win0, win1)
-    gs = max(owned // 2, 1)
-    groups = owned // gs
-    bounds = ((0, H - 16), (H - 16, S))
+    H = S // PARTS
+    win = (win0, win1, win2, win3)
+    edges = [0] + [h * H - 16 for h in range(1, PARTS)] + [S]
+    bounds = list(zip(edges[:-1], edges[1:]))
+    pair = 2 if owned % 2 == 0 else 1
 
     def var_copy(n):
         return pltpu.make_async_copy(
@@ -185,49 +188,47 @@
         (z > 0).astype(jnp.int32) + (z < Z - 1).astype(jnp.int32) + (X - 1) + (B - 1),
     )
 
-    def block(h, i):
-        return templates.at[0, pl.ds(i * gs, gs), pl.ds(h * H, H)]
-
-    def place(h, row, o, i):
-        return win[h].at[pl.ds(row * row_patches + column(o) * owned + i * gs, gs)]
-
-    def x_copy(h, o, i):
+    def block(h):
+        return templates.at[0, :, pl.ds(h * H, H)]
+
+    def place(h, row, o):
+        return win[h].at[pl.ds(row * row_patches + column(o) * owned, owned)]
+
+    def x_copy(h, o):
         return remote(
-            block(h, i),
-            place(h, 1, 0, i),
-            xs_sem.at[h, o, i],
-            xr_sem.at[h, o, i],
+            block(h),
+            place(h, 1, 0),
+            xs_sem.at[h, o],
+            xr_sem.at[h, o],
             {"patch": back_column(o)},
         )
 
-    def z_copy(h, d, o, i):
+    def z_copy(h, d, o):
         return remote(
-            block(h, i) if o == 0 else place(h, 1, o, i),
-            place(h, lands[d], o, i),
-            zs_sem.at[h, d, o, i],
-            zr_sem.at[h, d, o, i],
+            block(h) if o == 0 else place(h, 1, o),
+            place(h, lands[d], o),
+            zs_sem.at[h, d, o],
+            zr_sem.at[h, d, o],
             {"exp": target[d]},
         )
 
     def launch(h):
-        for i in range(groups):
-            for o in range(1, X):
-                x_copy(h, o, i).start()
+        for o in range(1, X):
+            x_copy(h, o).start()
+        for d in range(2):
+
+            @pl.when(to_exists[d])
+            def _():
+                z_copy(h, d, 0).start()
+
+    def forward(h):
+        for o in range(1, X):
+            x_copy(h, o).wait_recv()
             for d in range(2):
 
                 @pl.when(to_exists[d])
                 def _():
-                    z_copy(h, d, 0, i).start()
-
-    def forward(h):
-        for i in range(groups):
-            for o in range(1, X):
-                x_copy(h, o, i).wait_recv()
-                for d in range(2):
-
-                    @pl.when(to_exists[d])
-                    def _():
-                        z_copy(h, d, o, i).start()
+                    z_copy(h, d, o).start()
 
     def half_copy(buffer, send, recv, o, n):
         return remote(
@@ -248,29 +249,32 @@
         return carry
 
     launch(0)
+    launch(1)
 
     def start_exposure(n, carry):
         exp_copy(n).start()
         return carry
 
     lax.fori_loop(0, N, start_exposure, 0)
-    for h in range(2):
+    for h in range(PARTS):
         own_copy(h).start()
-    lax.fori_loop(0, N // 2, invert, 0)
+    lax.fori_loop(0, N, invert, 0)
     forward(0)
-    launch(1)
-    lax.fori_loop(N // 2, N, invert, 0)
-
-    count = len(profiles)
-    gcat[...] = jnp.zeros((S, 2 * count * H), jnp.bfloat16)
-    for p, table in enumerate(profile_tables(-offsets(H, H, 0))):
-        table = table.astype(jnp.bfloat16)
-        gcat[0:H, p * H : (p + 1) * H] = table
-        gcat[H:S, (count + p) * H : (count + p + 1) * H] = table
-    for p, table in enumerate(profile_tables(-offsets(16, H, -H))):
-        gcat[H : H + 16, p * H : (p + 1) * H] = table.astype(jnp.bfloat16)
-    for p, table in enumerate(profile_tables(-offsets(16, H, 16))):
-        gcat[H - 16 : H, (count + p) * H : (count + p + 1) * H] = table.astype(jnp.bfloat16)
+    launch(2)
+
+    count = len(profiles) + len(profiles) % 2
+    gcat[...] = jnp.zeros((S, PARTS * count * H), jnp.bfloat16)
+    row = lax.broadcasted_iota(jnp.int32, (H + 32, 2 * H), 0)
+    lane = lax.broadcasted_iota(jnp.int32, (H + 32, 2 * H), 1)
+    first_half = lane < H
+    tables = profile_tables(row - 16 - jnp.where(first_half, lane, lane - H))
+    tables = tables + [jnp.zeros_like(tables[0])] * (count - len(tables))
+    for p in range(0, count, 2):
+        table = jnp.where(first_half, tables[p], tables[p + 1]).astype(jnp.bfloat16)
+        for h in range(PARTS):
+            first, last = max(h * H - 16, 0), min((h + 1) * H + 16, S)
+            lanes = slice((h * count + p) * H, (h * count + p + 2) * H)
+            gcat[first:last, lanes] = table[first - h * H + 16 : last - h * H + 16]
     shifts = [(b - other_band(o)) * C for o in range(B)]
     for p, table in enumerate(profile_tables(offsets(C, C, 0))):
         gtab[p, 0:C, :] = table
@@ -299,16 +303,21 @@
                 start = C + (o - 1) * 32
                 mats[n, o * C : o * C + 16, lanes] = value[start : start + 16]
                 mats[n, (o + 1) * C - 16 : (o + 1) * C, lanes] = value[start + 16 : start + 32]
+        spare = count - len(profiles)
+        if spare:
+            mats[n, 0:C, (count - spare) * C :] = jnp.zeros((C, spare * C), jnp.bfloat16)
         return carry
 
+    forward(1)
+    launch(3)
     lax.fori_loop(0, N, mix, 0)
-    forward(1)
+    forward(2)
 
     for d in range(2):
 
         @pl.when(jnp.logical_not(from_exists[d]))
         def _():
-            for h in range(2):
+            for h in range(PARTS):
 
                 def clear(i, carry):
                     win[h][lands[d] * row_patches + i] = jnp.zeros((H, C), jnp.bfloat16)
@@ -323,14 +332,18 @@
             low[n, rows, lanes] = table.astype(jnp.bfloat16)
             square[n, rows, lanes] = (table * table).astype(jnp.bfloat16)
 
-        width = jnp.full((1, H), psf[0, e, 0, k], jnp.float32)
+        half = S // 2
+        width = jnp.full((1, half), psf[0, e, 0, k], jnp.float32)
         prow[n] = jnp.zeros((S, S), jnp.bfloat16)
         qrow[n] = jnp.zeros((S, S), jnp.bfloat16)
-        table = point_table(offsets(H, H, 0), width)
-        put(prow, qrow, slice(0, H), slice(0, H), table)
-        put(prow, qrow, slice(H, S), slice(H, S), table)
-        put(prow, qrow, slice(H, H + 16), slice(0, H), point_table(offsets(16, H, -H), width))
-        put(prow, qrow, slice(H - 16, H), slice(H, S), point_table(offsets(16, H, 16), width))
+        low, high = slice(0, half), slice(half, S)
+        table = point_table(offsets(half, half, 0), width)
+        put(prow, qrow, low, low, table)
+        put(prow, qrow, high, high, table)
+        table = point_table(offsets(16, half, -half), width)
+        put(prow, qrow, slice(half, half + 16), low, table)
+        table = point_table(offsets(16, half, 16), width)
+        put(prow, qrow, slice(half - 16, half), high, table)
         width = jnp.full((1, C), psf[0, e, 1, k], jnp.float32)
         pcol[n] = jnp.zeros((B * C, C), jnp.bfloat16)
         qcol[n] = jnp.zeros((B * C, C), jnp.bfloat16)
@@ -375,8 +388,7 @@
             @pl.when(from_exists[d])
             def _():
                 for o in range(X):
-                    for i in range(groups):
-                        z_copy(h, d, o, i).wait_recv()
+                    z_copy(h, d, o).wait_recv()
 
     def tile_copy(h, o, n):
         return remote(
@@ -389,7 +401,7 @@
 
     def middle(h):
         first, last = bounds[h]
-        depth = (h + 1) * count * H
+        start, end = max(h - 1, 0) * count * H, (h + 1) * count * H
 
         def choose(n, carry):
             tfull[h, n, :, 0:C] = win[h][ids[0, n // slots, lax.rem(n, slots)]]
@@ -420,8 +432,8 @@
                             :, v * C : (v + 1) * C
                         ]
             convolved = jnp.dot(
-                gcat[first:last, 0:depth],
-                cols[pair, 0:depth, :],
+                gcat[first:last, start:end],
+                cols[pair, start:end, :],
                 preferred_element_type=jnp.float32,
             )
             for a in range(2):
@@ -430,7 +442,7 @@
                 value = (value - convolved[:, a * C : (a + 1) * C]) * inv[n, first:last, :]
                 wval[n, first:last, :] = value
                 wfull[n, first:last, 0:C] = value.astype(jnp.bfloat16)
-                if h == 1:
+                if h == PARTS - 1:
                     for o in range(1, B):
                         half_copy(wfull, ws_sem, wr_sem, o, n).start()
             return carry
@@ -457,34 +469,36 @@
 
     def p_copy(h, d, q, t):
         first, last = bounds[h]
-        rows = pl.ds(first, last - first)
+        part = (d, pl.ds(q, pair), pl.ds(first, last - first))
         return remote(
-            psend.at[d, q, rows],
-            precv.at[d, q, rows],
+            psend.at[part],
+            precv.at[part],
             ps_sem.at[h, d, t],
             pr_sem.at[h, d, t],
             {"exp": target[d]},
         )
 
     def patch_of(t):
-        return lax.rem(x + 1 + t // owned, X) * owned + lax.rem(t, owned)
+        per = owned // pair
+        return lax.rem(x + 1 + t // per, X) * owned + lax.rem(t, per) * pair
 
     def push(h):
         def step(t, carry):
-            q = patch_of(t)
-            for rows, (up, own, down) in partials(h, q, (0, 1, 2)):
-                psend[0, q, rows, :] = up.astype(jnp.bfloat16)
-                psend[1, q, rows, :] = down.astype(jnp.bfloat16)
-                pown[q, rows, :] = own
+            for v in range(pair):
+                q = patch_of(t) + v
+                for rows, (up, own, down) in partials(h, q, (0, 1, 2)):
+                    psend[0, q, rows, :] = up.astype(jnp.bfloat16)
+                    psend[1, q, rows, :] = down.astype(jnp.bfloat16)
+                    pown[q, rows, :] = own
             for d in range(2):
 
                 @pl.when(to_exists[d])
                 def _():
-                    p_copy(h, d, q, t).start()
+                    p_copy(h, d, patch_of(t), t).start()
 
             return carry
 
-        lax.fori_loop(0, row_patches, step, 0)
+        lax.fori_loop(0, row_patches // pair, step, 0)
 
     def numerator(pair, carry):
         tiles = (pair * 2, pair * 2 + 1)
@@ -496,85 +510,99 @@
             score[0, n // slots, lax.rem(n, slots)] = result * rden[n]
         return carry
 
-    def gather_rows(h, t, q):
+    def gather_rows(h, o):
         first, last = bounds[h]
-        for d in range(2):
-
-            @pl.when(from_exists[d])
-            def _():
-                p_copy(h, d, q, t).wait_recv()
-                pown[q, first:last, :] += precv[d, q, first:last, :].astype(jnp.float32)
-
-    def s_copy(h, s, i):
+        for i in range(0, owned, pair):
+            t = ((o + X - 1) % X) * (owned // pair) + i // pair
+            q = column(o) * owned + i
+            for d in range(2):
+
+                @pl.when(from_exists[d])
+                def _():
+                    p_copy(h, d, q, t).wait_recv()
+                    for v in range(pair):
+                        extra = precv[d, q + v, first:last, :].astype(jnp.float32)
+                        pown[q + v, first:last, :] += extra
+
+    def s_copy(h, s):
         first, last = bounds[h]
         rows = pl.ds(first, last - first)
         return remote(
-            xsend.at[s, i, rows],
-            xrecv.at[s, i, rows],
-            ss_sem.at[h, s, i],
-            sr_sem.at[h, s, i],
+            xsend.at[s, :, rows],
+            xrecv.at[s, :, rows],
+            ss_sem.at[h, s],
+            sr_sem.at[h, s],
             {"patch": column(s + 1)},
         )
 
     def pass_on(h):
         first, last = bounds[h]
         for s in range(X - 1):
+            gather_rows(h, s + 1)
             for i in range(owned):
                 q = column(s + 1) * owned + i
-                gather_rows(h, s * owned + i, q)
                 xsend[s, i, first:last, :] = pown[q, first:last, :].astype(jnp.bfloat16)
-                s_copy(h, s, i).start()
+            s_copy(h, s).start()
 
     def finish_sums(h):
         first, last = bounds[h]
+        gather_rows(h, 0)
+        for s in range(X - 1):
+            s_copy(h, s).wait_recv()
         for i in range(owned):
-            q = x * owned + i
-            gather_rows(h, (X - 1) * owned + i, q)
-            value = pown[q, first:last, :]
+            value = pown[x * owned + i, first:last, :]
             for s in range(X - 1):
-                s_copy(h, s, i).wait_recv()
                 value = value + xrecv[s, i, first:last, :].astype(jnp.float32)
             coadd[0, i, first:last, :] = value
 
     arrive(0)
     middle(0)
     push(0)
-    lax.fori_loop(0, N, spread, 0)
+    forward(3)
+    lax.fori_loop(0, N // 2, spread, 0)
     arrive(1)
     middle(1)
     push(1)
     pass_on(0)
-    lax.fori_loop(0, N // 2, denominator, 0)
+    lax.fori_loop(N // 2, N, spread, 0)
+    arrive(2)
+    middle(2)
+    push(2)
     pass_on(1)
     finish_sums(0)
+    arrive(3)
+    middle(3)
+    push(3)
+    pass_on(2)
+    lax.fori_loop(0, N // 2, denominator, 0)
+    pass_on(3)
+    finish_sums(1)
+    finish_sums(2)
     lax.fori_loop(0, N // 2, numerator, 0)
-    finish_sums(1)
-
-    for h in range(2):
+    finish_sums(3)
+
+    for h in range(PARTS):
         for o in range(1, X):
-            for i in range(groups):
-                x_copy(h, o, i).wait_send()
-            for i in range(owned):
-                s_copy(h, o - 1, i).wait_send()
+            x_copy(h, o).wait_send()
+            s_copy(h, o - 1).wait_send()
         for d in range(2):
 
             @pl.when(to_exists[d])
             def _():
                 for o in range(X):
-                    for i in range(groups):
-                        z_copy(h, d, o, i).wait_send()
+                    z_copy(h, d, o).wait_send()
 
                 def sent(t, carry):
                     p_copy(h, d, patch_of(t), t).wait_send()
                     return carry
 
-                lax.fori_loop(0, row_patches, sent, 0)
+                lax.fori_loop(0, row_patches // pair, sent, 0)
 
     def finish(n, carry):
         for o in range(1, B):
             half_copy(ifull, is_sem, ir_sem, o, n).wait_send()
             half_copy(wfull, ws_sem, wr_sem, o, n).wait_send()
-            for h in range(2):
+            for h in range(PARTS):
                 tile_copy(h, o, n).wait_send()
         return carry
 
@@ -586,13 +614,12 @@
     Z, X, B = (lax.axis_size(axis) for axis in ("exp", "patch", "band"))
     N = patch_ids.shape[1] * patch_ids.shape[2]
     row = X * owned
-    count = len(profiles)
+    count = len(profiles) + len(profiles) % 2
     bf16, f32 = jnp.bfloat16, jnp.float32
     dma = pltpu.SemaphoreType.DMA
     scratch = [
-        pltpu.VMEM((3 * row, S // 2, C), bf16),
-        pltpu.VMEM((3 * row, S // 2, C), bf16),
-        pltpu.VMEM((2, N, S // 2, B * C), bf16),
+        *[pltpu.VMEM((3 * row, S // PARTS, C), bf16) for _ in range(PARTS)],
+        pltpu.VMEM((PARTS, N, S // PARTS, B * C), bf16),
         pltpu.VMEM((N, B * C, count * C), bf16),
         pltpu.VMEM((S, count * S), bf16),
         pltpu.VMEM((count, C + 32 * (B - 1), C), f32),
@@ -612,23 +639,23 @@
         pltpu.VMEM((row, S, C), f32),
         pltpu.VMEM((max(X - 1, 1), owned, S, C), bf16),
         pltpu.VMEM((max(X - 1, 1), owned, S, C), bf16),
-        dma((2,)),
+        dma((PARTS,)),
         dma((N,)),
         dma((N,)),
-        dma((2, X, owned)),
-        dma((2, X, owned)),
-        dma((2, 2, X, owned)),
-        dma((2, 2, X, owned)),
-        dma((2, B, N)),
-        dma((2, B, N)),
+        dma((PARTS, X)),
+        dma((PARTS, X)),
+        dma((PARTS, 2, X)),
+        dma((PARTS, 2, X)),
+        dma((PARTS, B, N)),
+        dma((PARTS, B, N)),
         dma((B, N)),
         dma((B, N)),
         dma((B, N)),
         dma((B, N)),
-        dma((2, 2, row)),
-        dma((2, 2, row)),
-        dma((2, max(X - 1, 1), owned)),
-        dma((2, max(X - 1, 1), owned)),
+        dma((PARTS, 2, row)),
+        dma((PARTS, 2, row)),
+        dma((PARTS, max(X - 1, 1))),
+        dma((PARTS, max(X - 1, 1))),
     ]
     any_spec = pl.BlockSpec(memory_space=pl.ANY)
     vmem = pl.BlockSpec(memory_space=pltpu.VMEM)

time: 39 us -> 45.7 us (1.17)
  Pallas kernels: 36.5 us -> 43.1 us
    pallas_call x1, Pallas kernels: 36.5 us -> 43.1 us  [on_device(): pl.pallas_call(functools.partial(kernel, (Z, X, B)), out_shape=(pltpu.VME...]
where the time goes in v4:
time: 45.7 us; the launch traced here: 45.5 us
  Pallas kernels  43.1 us (94%)
  local copies, waits for them, and re-layouts  1.77 us (4%)
  between operations  0.64 us (1%)
    pallas_call x1, Pallas kernels, on_device(): pl.pallas_call(functools.partial(kernel, (Z, X, B)), out_shape=(pltpu.VME...  43.1 us
    unnamed x2, local copies, waits for them, and re-layouts  1.77 us

profile of v4, /device:TPU:0, one launch (start us, length us, event | category | flops | bytes accessed | tf_op | source)
XLA Modules:
  0.0 45.5 jit_solution(2027587047857921817)
XLA Ops:
  0.6 43.1 %shard_map.86 = (f32[1,4,256,128]{3,2,1,0:T(8,128)S(1)}, f32[1,2,4,256,128]{4,3,2,1,0:T(8,128)S(1)}) custom-call(bf16[1,4,256,128]{3,2,1,0:T(8,128)(2,1)} %templates.1, bf16[1,2,4,256,128]{4,3,2,1,0:T(8,128)(2,1)} %exposures.1, f32[1,2,4,256,128]{4,3,2,1,0:T(8,128)} %variance.1, f32[1,2,4,27]{3,2,1,0:T(4,128)} %coeff.1, f32[1,2,2,4]{3,2,1,0:T(2,128)} %bitcast.1, ...), custom_call_target="tpu_custom_call" | custom-call | tf_op jit(solution)/shard_map/pallas_call | solution.py:663
  43.7 0.8 %copy.11 = f32[1,4,256,128]{3,2,1,0:T(8,128)} copy(f32[1,4,256,128]{3,2,1,0:T(8,128)S(1)} %get-tuple-element.2) | data formatting | bytes 1048576
  44.5 1.0 %copy.12 = f32[1,2,4,256,128]{4,3,2,1,0:T(8,128)} copy(f32[1,2,4,256,128]{4,3,2,1,0:T(8,128)S(1)} %get-tuple-element.3) | data formatting | bytes 2097152

commit v5 on v3

--- a/solution.py
+++ b/solution.py
@@ -358,8 +358,8 @@
             for part, chain in zip(middle, chains)
         ]
 
-    def denominator(pair, carry):
-        tiles = (pair * 2, pair * 2 + 1)
+    def denominator(step, carry):
+        tiles = [step * 4 + a for a in range(4)]
         for n in tiles:
             for o in range(1, B):
                 half_copy(ifull, is_sem, ir_sem, o, n).wait_recv()
@@ -397,28 +397,26 @@
                 tile_copy(h, o, n).start()
             return carry
 
-        lax.fori_loop(0, N, choose, 0)
-
-        def convolve(pair, carry):
-            for a in range(2):
-                n = pair * 2 + a
-                if h == 0:
-                    exp_copy(n).wait()
-                for o in range(1, B):
-                    tile_copy(h, o, n).wait_recv()
-                tile = tfull[h, n]
-                for p in range(0, count, 2):
-                    wide = min(2, count - p)
-                    part = jnp.dot(
-                        tile,
-                        mats[n, :, p * C : (p + wide) * C],
-                        preferred_element_type=jnp.float32,
-                    ).astype(jnp.bfloat16)
-                    for v in range(wide):
-                        row = (h * count + p + v) * H
-                        cols[pair, row : row + H, a * C : (a + 1) * C] = part[
-                            :, v * C : (v + 1) * C
-                        ]
+        for n in range(N):
+            choose(n, 0)
+        for n in range(N):
+            if h == 0:
+                exp_copy(n).wait()
+            for o in range(1, B):
+                tile_copy(h, o, n).wait_recv()
+            tile = tfull[h, n]
+            pair, a = n // 2, n % 2
+            for p in range(0, count, 2):
+                wide = min(2, count - p)
+                part = jnp.dot(
+                    tile,
+                    mats[n, :, p * C : (p + wide) * C],
+                    preferred_element_type=jnp.float32,
+                ).astype(jnp.bfloat16)
+                for v in range(wide):
+                    row = (h * count + p + v) * H
+                    cols[pair, row : row + H, a * C : (a + 1) * C] = part[:, v * C : (v + 1) * C]
+        for pair in range(N // 2):
             convolved = jnp.dot(
                 gcat[first:last, 0:depth],
                 cols[pair, 0:depth, :],
@@ -433,9 +431,6 @@
                 if h == 1:
                     for o in range(1, B):
                         half_copy(wfull, ws_sem, wr_sem, o, n).start()
-            return carry
-
-        lax.fori_loop(0, N // 2, convolve, 0)
 
     def partials(h, q, rows):
         first, last = bounds[h]
@@ -486,8 +481,8 @@
 
         lax.fori_loop(0, row_patches, step, 0)
 
-    def numerator(pair, carry):
-        tiles = (pair * 2, pair * 2 + 1)
+    def numerator(step, carry):
+        tiles = [step * 4 + a for a in range(4)]
         for n in tiles:
             for o in range(1, B):
                 half_copy(wfull, ws_sem, wr_sem, o, n).wait_recv()
@@ -539,15 +534,15 @@
     arrive(0)
     middle(0)
     push(0)
-    lax.fori_loop(0, N, spread, 0)
     arrive(1)
     middle(1)
     push(1)
     pass_on(0)
-    lax.fori_loop(0, N // 2, denominator, 0)
+    lax.fori_loop(0, N, spread, 0)
+    lax.fori_loop(0, N // 4, denominator, 0)
     pass_on(1)
     finish_sums(0)
-    lax.fori_loop(0, N // 2, numerator, 0)
+    lax.fori_loop(0, N // 4, numerator, 0)
     finish_sums(1)
 
     for h in range(2):

time: 39 us -> 38.4 us (0.985)
  Pallas kernels: 36.5 us -> 35.9 us
    pallas_call x1, Pallas kernels: 36.5 us -> 35.9 us  [on_device(): pl.pallas_call(functools.partial(kernel, (Z, X, B)), out_shape=(pltpu.VME...]
where the time goes in v5:
time: 38.4 us; the launch traced here: 38.3 us
  Pallas kernels  35.9 us (93%)
  local copies, waits for them, and re-layouts  1.77 us (5%)
  between operations  0.64 us (2%)
    pallas_call x1, Pallas kernels, on_device(): pl.pallas_call(functools.partial(kernel, (Z, X, B)), out_shape=(pltpu.VME...  35.9 us
    unnamed x2, local copies, waits for them, and re-layouts  1.77 us

profile of v5, /device:TPU:0, one launch (start us, length us, event | category | flops | bytes accessed | tf_op | source)
XLA Modules:
  0.0 38.3 jit_solution(14536163814502520887)
XLA Ops:
  0.6 35.9 %shard_map.86 = (f32[1,4,256,128]{3,2,1,0:T(8,128)S(1)}, f32[1,2,4,256,128]{4,3,2,1,0:T(8,128)S(1)}) custom-call(bf16[1,4,256,128]{3,2,1,0:T(8,128)(2,1)} %templates.1, bf16[1,2,4,256,128]{4,3,2,1,0:T(8,128)(2,1)} %exposures.1, f32[1,2,4,256,128]{4,3,2,1,0:T(8,128)} %variance.1, f32[1,2,4,27]{3,2,1,0:T(4,128)} %coeff.1, f32[1,2,2,4]{3,2,1,0:T(2,128)} %bitcast.1, ...), custom_call_target="tpu_custom_call" | custom-call | tf_op jit(solution)/shard_map/pallas_call | solution.py:631
  36.5 0.8 %copy.11 = f32[1,4,256,128]{3,2,1,0:T(8,128)} copy(f32[1,4,256,128]{3,2,1,0:T(8,128)S(1)} %get-tuple-element.2) | data formatting | bytes 1048576
  37.3 1.0 %copy.12 = f32[1,2,4,256,128]{4,3,2,1,0:T(8,128)} copy(f32[1,2,4,256,128]{4,3,2,1,0:T(8,128)S(1)} %get-tuple-element.3) | data formatting | bytes 2097152

commit v6 on v5

--- a/solution.py
+++ b/solution.py
@@ -103,6 +103,11 @@
     pr_sem,
     ss_sem,
     sr_sem,
+    frecv,
+    ys_sem,
+    yr_sem,
+    fs_sem,
+    fr_sem,
 ):
     Z, X, B = sizes
     owned, S, C = templates.shape[1:]
@@ -157,6 +162,12 @@
     gs = max(owned // 2, 1)
     groups = owned // gs
     bounds = ((0, H - 16), (H - 16, S))
+    relayed = groups > 1 and X > 1
+    near = owned - gs if relayed else owned
+
+    def turns(h, i):
+        return relayed and h == 0 and i == groups - 1
+
 
     def var_copy(n):
         return pltpu.make_async_copy(
@@ -209,10 +220,17 @@
             {"exp": target[d]},
         )
 
-    def launch(h):
+    def y_copy(d, o):
+        part = place(0, lands[d], 0, groups - 1)
+        return remote(part, part, ys_sem.at[d, o], yr_sem.at[d, o], {"patch": back_column(o)})
+
+    def launch_x(h):
         for i in range(groups):
             for o in range(1, X):
                 x_copy(h, o, i).start()
+
+    def launch_z(h):
+        for i in reversed(range(groups)):
             for d in range(2):
 
                 @pl.when(to_exists[d])
@@ -223,11 +241,24 @@
         for i in range(groups):
             for o in range(1, X):
                 x_copy(h, o, i).wait_recv()
+                if turns(h, i):
+                    continue
                 for d in range(2):
 
                     @pl.when(to_exists[d])
                     def _():
                         z_copy(h, d, o, i).start()
+
+    def relay():
+        if not relayed:
+            return
+        for d in range(2):
+
+            @pl.when(from_exists[d])
+            def _():
+                z_copy(0, d, 0, groups - 1).wait_recv()
+                for o in range(1, X):
+                    y_copy(d, o).start()
 
     def half_copy(buffer, send, recv, o, n):
         return remote(
@@ -247,7 +278,8 @@
             half_copy(ifull, is_sem, ir_sem, o, n).start()
         return carry
 
-    launch(0)
+    launch_x(0)
+    launch_z(0)
 
     def start_exposure(n, carry):
         exp_copy(n).start()
@@ -256,10 +288,11 @@
     lax.fori_loop(0, N, start_exposure, 0)
     for h in range(2):
         own_copy(h).start()
-    lax.fori_loop(0, N // 2, invert, 0)
+    lax.fori_loop(0, N, invert, 0)
     forward(0)
-    launch(1)
-    lax.fori_loop(N // 2, N, invert, 0)
+    launch_z(1)
+    relay()
+    launch_x(1)
 
     count = len(profiles)
     gcat[...] = jnp.zeros((S, 2 * count * H), jnp.bfloat16)
@@ -376,7 +409,10 @@
             def _():
                 for o in range(X):
                     for i in range(groups):
-                        z_copy(h, d, o, i).wait_recv()
+                        if not turns(h, i):
+                            z_copy(h, d, o, i).wait_recv()
+                        elif o > 0:
+                            y_copy(d, o).wait_recv()
 
     def tile_copy(h, o, n):
         return remote(
@@ -461,25 +497,71 @@
             {"exp": target[d]},
         )
 
-    def patch_of(t):
-        return lax.rem(x + 1 + t // owned, X) * owned + lax.rem(t, owned)
+    def f_copy(d, s, i):
+        first, last = bounds[0]
+        rows = pl.ds(first, last - first)
+        return remote(
+            psend.at[d, column(s + 1) * owned + i, rows],
+            frecv.at[d, s, i - near, rows],
+            fs_sem.at[d, s, i - near],
+            fr_sem.at[d, s, i - near],
+            {"patch": column(s + 1)},
+        )
 
     def push(h):
-        def step(t, carry):
-            q = patch_of(t)
+        first, last = bounds[h]
+        limit = near if h == 0 else owned
+
+        def fill(q):
             for rows, (up, own, down) in partials(h, q, (0, 1, 2)):
                 psend[0, q, rows, :] = up.astype(jnp.bfloat16)
                 psend[1, q, rows, :] = down.astype(jnp.bfloat16)
                 pown[q, rows, :] = own
+
+        def along(t, carry):
+            s, i = t // gs, near + lax.rem(t, gs)
+            fill(column(s + 1) * owned + i)
             for d in range(2):
 
                 @pl.when(to_exists[d])
                 def _():
-                    p_copy(h, d, q, t).start()
+                    f_copy(d, s, i).start()
 
             return carry
 
-        lax.fori_loop(0, row_patches, step, 0)
+        def step(t, carry):
+            s, i = t // limit, lax.rem(t, limit)
+            q = column(s + 1) * owned + i
+            fill(q)
+            for d in range(2):
+
+                @pl.when(to_exists[d])
+                def _():
+                    p_copy(h, d, q, s * owned + i).start()
+
+            return carry
+
+        def joined(i, carry):
+            q = x * owned + i
+            fill(q)
+            for d in range(2):
+
+                @pl.when(to_exists[d])
+                def _():
+                    value = psend[d, q, first:last, :].astype(jnp.float32)
+                    for s in range(X - 1):
+                        f_copy(d, s, i).wait_recv()
+                        value = value + frecv[d, s, i - near, first:last, :].astype(jnp.float32)
+                    psend[d, q, first:last, :] = value.astype(jnp.bfloat16)
+                    p_copy(h, d, q, (X - 1) * owned + i).start()
+
+            return carry
+
+        if limit < owned:
+            lax.fori_loop(0, (X - 1) * gs, along, 0)
+        lax.fori_loop(0, X * limit, step, 0)
+        if limit < owned:
+            lax.fori_loop(limit, owned, joined, 0)
 
     def numerator(step, carry):
         tiles = [step * 4 + a for a in range(4)]
@@ -516,7 +598,8 @@
         for s in range(X - 1):
             for i in range(owned):
                 q = column(s + 1) * owned + i
-                gather_rows(h, s * owned + i, q)
+                if h == 1 or i < near:
+                    gather_rows(h, s * owned + i, q)
                 xsend[s, i, first:last, :] = pown[q, first:last, :].astype(jnp.bfloat16)
                 s_copy(h, s, i).start()
 
@@ -557,13 +640,21 @@
             def _():
                 for o in range(X):
                     for i in range(groups):
-                        z_copy(h, d, o, i).wait_send()
-
-                def sent(t, carry):
-                    p_copy(h, d, patch_of(t), t).wait_send()
-                    return carry
-
-                lax.fori_loop(0, row_patches, sent, 0)
+                        if o == 0 or not turns(h, i):
+                            z_copy(h, d, o, i).wait_send()
+                for s in range(X):
+                    for i in range(owned):
+                        if h == 1 or s == X - 1 or i < near:
+                            p_copy(h, d, column(s + 1) * owned + i, s * owned + i).wait_send()
+                        else:
+                            f_copy(d, s, i).wait_send()
+
+            if relayed and h == 0:
+
+                @pl.when(from_exists[d])
+                def _():
+                    for o in range(1, X):
+                        y_copy(d, o).wait_send()
 
     def finish(n, carry):
         for o in range(1, B):
@@ -624,6 +715,11 @@
         dma((2, 2, row)),
         dma((2, max(X - 1, 1), owned)),
         dma((2, max(X - 1, 1), owned)),
+        pltpu.VMEM((2, max(X - 1, 1), max(owned // 2, 1), S, C), bf16),
+        dma((2, X)),
+        dma((2, X)),
+        dma((2, max(X - 1, 1), max(owned // 2, 1))),
+        dma((2, max(X - 1, 1), max(owned // 2, 1))),
     ]
     any_spec = pl.BlockSpec(memory_space=pl.ANY)
     vmem = pl.BlockSpec(memory_space=pltpu.VMEM)

time: 38.4 us -> 43 us (1.12)
  Pallas kernels: 35.9 us -> 40.4 us
    pallas_call x1, Pallas kernels: 35.9 us -> 40.4 us  [on_device(): pl.pallas_call(functools.partial(kernel, (Z, X, B)), out_shape=(pltpu.VME...]
where the time goes in v6:
time: 43 us; the launch traced here: 42.8 us
  Pallas kernels  40.4 us (94%)
  local copies, waits for them, and re-layouts  1.77 us (4%)
  between operations  0.64 us (1%)
    pallas_call x1, Pallas kernels, on_device(): pl.pallas_call(functools.partial(kernel, (Z, X, B)), out_shape=(pltpu.VME...  40.4 us
    unnamed x2, local copies, waits for them, and re-layouts  1.77 us

profile of v6, /device:TPU:0, one launch (start us, length us, event | category | flops | bytes accessed | tf_op | source)
XLA Modules:
  0.0 42.8 jit_solution(10382816240176911046)
XLA Ops:
  0.6 40.4 %shard_map.86 = (f32[1,4,256,128]{3,2,1,0:T(8,128)S(1)}, f32[1,2,4,256,128]{4,3,2,1,0:T(8,128)S(1)}) custom-call(bf16[1,4,256,128]{3,2,1,0:T(8,128)(2,1)} %templates.1, bf16[1,2,4,256,128]{4,3,2,1,0:T(8,128)(2,1)} %exposures.1, f32[1,2,4,256,128]{4,3,2,1,0:T(8,128)} %variance.1, f32[1,2,4,27]{3,2,1,0:T(4,128)} %coeff.1, f32[1,2,2,4]{3,2,1,0:T(2,128)} %bitcast.1, ...), custom_call_target="tpu_custom_call" | custom-call | tf_op jit(solution)/shard_map/pallas_call | solution.py:727
  41.0 0.8 %copy.11 = f32[1,4,256,128]{3,2,1,0:T(8,128)} copy(f32[1,4,256,128]{3,2,1,0:T(8,128)S(1)} %get-tuple-element.2) | data formatting | bytes 1048576
  41.8 1.0 %copy.12 = f32[1,2,4,256,128]{4,3,2,1,0:T(8,128)} copy(f32[1,2,4,256,128]{4,3,2,1,0:T(8,128)S(1)} %get-tuple-element.3) | data formatting | bytes 2097152

commit v7 on v5

--- a/solution.py
+++ b/solution.py
@@ -209,10 +209,13 @@
             {"exp": target[d]},
         )
 
-    def launch(h):
+    def launch_x(h):
         for i in range(groups):
             for o in range(1, X):
                 x_copy(h, o, i).start()
+
+    def launch_z(h):
+        for i in range(groups):
             for d in range(2):
 
                 @pl.when(to_exists[d])
@@ -247,7 +250,9 @@
             half_copy(ifull, is_sem, ir_sem, o, n).start()
         return carry
 
-    launch(0)
+    launch_x(0)
+    launch_z(0)
+    launch_x(1)
 
     def start_exposure(n, carry):
         exp_copy(n).start()
@@ -258,7 +263,7 @@
         own_copy(h).start()
     lax.fori_loop(0, N // 2, invert, 0)
     forward(0)
-    launch(1)
+    launch_z(1)
     lax.fori_loop(N // 2, N, invert, 0)
 
     count = len(profiles)
@@ -301,8 +306,8 @@
                 mats[n, (o + 1) * C - 16 : (o + 1) * C, lanes] = value[start + 16 : start + 32]
         return carry
 
+    forward(1)
     lax.fori_loop(0, N, mix, 0)
-    forward(1)
 
     for d in range(2):
 
@@ -539,8 +544,9 @@
     push(1)
     pass_on(0)
     lax.fori_loop(0, N, spread, 0)
-    lax.fori_loop(0, N // 4, denominator, 0)
+    denominator(0, 0)
     pass_on(1)
+    lax.fori_loop(1, N // 4, denominator, 0)
     finish_sums(0)
     lax.fori_loop(0, N // 4, numerator, 0)
     finish_sums(1)

time: 38.4 us -> 39 us (1.016)
  Pallas kernels: 35.9 us -> 36.4 us
    pallas_call x1, Pallas kernels: 35.9 us -> 36.4 us  [on_device(): pl.pallas_call(functools.partial(kernel, (Z, X, B)), out_shape=(pltpu.VME...]
where the time goes in v7:
time: 39 us; the launch traced here: 38.8 us
  Pallas kernels  36.4 us (93%)
  local copies, waits for them, and re-layouts  1.77 us (5%)
  between operations  0.64 us (2%)
    pallas_call x1, Pallas kernels, on_device(): pl.pallas_call(functools.partial(kernel, (Z, X, B)), out_shape=(pltpu.VME...  36.4 us
    unnamed x2, local copies, waits for them, and re-layouts  1.77 us

profile of v7, /device:TPU:0, one launch (start us, length us, event | category | flops | bytes accessed | tf_op | source)
XLA Modules:
  0.0 38.8 jit_solution(3451266644602971847)
XLA Ops:
  0.6 36.4 %shard_map.86 = (f32[1,4,256,128]{3,2,1,0:T(8,128)S(1)}, f32[1,2,4,256,128]{4,3,2,1,0:T(8,128)S(1)}) custom-call(bf16[1,4,256,128]{3,2,1,0:T(8,128)(2,1)} %templates.1, bf16[1,2,4,256,128]{4,3,2,1,0:T(8,128)(2,1)} %exposures.1, f32[1,2,4,256,128]{4,3,2,1,0:T(8,128)} %variance.1, f32[1,2,4,27]{3,2,1,0:T(4,128)} %coeff.1, f32[1,2,2,4]{3,2,1,0:T(2,128)} %bitcast.1, ...), custom_call_target="tpu_custom_call" | custom-call | tf_op jit(solution)/shard_map/pallas_call | solution.py:637
  37.0 0.8 %copy.11 = f32[1,4,256,128]{3,2,1,0:T(8,128)} copy(f32[1,4,256,128]{3,2,1,0:T(8,128)S(1)} %get-tuple-element.2) | data formatting | bytes 1048576
  37.8 1.0 %copy.12 = f32[1,2,4,256,128]{4,3,2,1,0:T(8,128)} copy(f32[1,2,4,256,128]{4,3,2,1,0:T(8,128)S(1)} %get-tuple-element.3) | data formatting | bytes 2097152

commit v8 on v7

--- a/solution.py
+++ b/solution.py
@@ -539,14 +539,14 @@
     arrive(0)
     middle(0)
     push(0)
+    lax.fori_loop(0, N, spread, 0)
+    denominator(0, 0)
     arrive(1)
     middle(1)
     push(1)
     pass_on(0)
-    lax.fori_loop(0, N, spread, 0)
-    denominator(0, 0)
+    lax.fori_loop(1, N // 4, denominator, 0)
     pass_on(1)
-    lax.fori_loop(1, N // 4, denominator, 0)
     finish_sums(0)
     lax.fori_loop(0, N // 4, numerator, 0)
     finish_sums(1)

time: 39 us -> 40.1 us (1.028)
  Pallas kernels: 36.4 us -> 37.5 us
    pallas_call x1, Pallas kernels: 36.4 us -> 37.5 us  [on_device(): pl.pallas_call(functools.partial(kernel, (Z, X, B)), out_shape=(pltpu.VME...]
where the time goes in v8:
time: 40.1 us; the launch traced here: 39.9 us
  Pallas kernels  37.5 us (94%)
  local copies, waits for them, and re-layouts  1.77 us (4%)
  between operations  0.64 us (2%)
    pallas_call x1, Pallas kernels, on_device(): pl.pallas_call(functools.partial(kernel, (Z, X, B)), out_shape=(pltpu.VME...  37.5 us
    unnamed x2, local copies, waits for them, and re-layouts  1.77 us

profile of v8, /device:TPU:0, one launch (start us, length us, event | category | flops | bytes accessed | tf_op | source)
XLA Modules:
  0.0 39.9 jit_solution(512285369584766061)
XLA Ops:
  0.6 37.5 %shard_map.86 = (f32[1,4,256,128]{3,2,1,0:T(8,128)S(1)}, f32[1,2,4,256,128]{4,3,2,1,0:T(8,128)S(1)}) custom-call(bf16[1,4,256,128]{3,2,1,0:T(8,128)(2,1)} %templates.1, bf16[1,2,4,256,128]{4,3,2,1,0:T(8,128)(2,1)} %exposures.1, f32[1,2,4,256,128]{4,3,2,1,0:T(8,128)} %variance.1, f32[1,2,4,27]{3,2,1,0:T(4,128)} %coeff.1, f32[1,2,2,4]{3,2,1,0:T(2,128)} %bitcast.1, ...), custom_call_target="tpu_custom_call" | custom-call | tf_op jit(solution)/shard_map/pallas_call | solution.py:637
  38.2 0.8 %copy.11 = f32[1,4,256,128]{3,2,1,0:T(8,128)} copy(f32[1,4,256,128]{3,2,1,0:T(8,128)S(1)} %get-tuple-element.2) | data formatting | bytes 1048576
  39.0 1.0 %copy.12 = f32[1,2,4,256,128]{4,3,2,1,0:T(8,128)} copy(f32[1,2,4,256,128]{4,3,2,1,0:T(8,128)S(1)} %get-tuple-element.3) | data formatting | bytes 2097152
